TPU v7x, 256 devices: a whole 4x4x8 slice. The times are simulated.
256 devices in a mesh: dp: 128 (over x, y, z), helper: 2 (over core).
Axes of the slice: x: 4, y: 4, z: 8, core: 2. Of those that a mesh axis runs over, the one named last changes fastest.
Arguments:
- embedding: bfloat16 [98304, 1024], P(('dp', 'helper'))
- cluster: int32 [98304], P(('dp', 'helper')), may hold values from 0 to 511, as said below
- member_order: int32 [98304], P(('dp', 'helper')), may hold values from 0 to 98303, each once
Outputs:
- nearest: float32 [98304], P(('dp', 'helper'))
Inputs may be any that keep to these rules, and one draw needn't show every extreme that they name: The owner of a cluster c is c mod 128; among the documents of one device at most 6 have the same owner, and on every device some owner has exactly 6. `member_order`: each value appears once.
All inputs are finite; a program needn't handle non-finite values.
Results may differ from a plain program's by a relative error of at most 0.0005.
Values may be sent and summed in bfloat16 or wider, within the bound.
No kernel may reach another device: no remote copies, remote signals or barrier semaphores. Data moves between devices by JAX's collectives and lax.ppermute only.
A program may use at most 64 MiB of HBM per device.

v0:
```python
import jax
import jax.numpy as jnp
from jax import lax
from jax.sharding import PartitionSpec as P


def normalize(embedding):
    values = embedding.astype(jnp.float32)
    return (values * lax.rsqrt(jnp.sum(values * values, axis=1, keepdims=True) + 1e-06)).astype(
        jnp.bfloat16
    )


def slot_index(owner, owners, capacity):
    columns = jnp.arange(owners, dtype=jnp.int32)
    matches = (owner[:, None] == columns[None, :]).astype(jnp.int32)
    earlier = jnp.cumsum(matches, axis=0) - matches
    return owner * capacity + jnp.sum(earlier * matches, axis=1)


def pack_rows(normed, cluster, member_order, target, owners, capacity):
    feature = normed.shape[1]
    slot_total = owners * capacity
    packed = jnp.zeros((slot_total, feature), jnp.bfloat16).at[target].set(normed)
    labels = jnp.full((slot_total,), -1, jnp.int32).at[target].set(cluster)
    ranks = jnp.zeros((slot_total,), jnp.int32).at[target].set(member_order)
    return (
        packed.reshape(owners, capacity, feature),
        labels.reshape(owners, capacity),
        ranks.reshape(owners, capacity),
    )


def best_earlier(queries, query_label, query_rank, key_rows, key_label, key_rank):
    scores = lax.dot_general(
        queries, key_rows, (((1,), (1,)), ((), ())), preferred_element_type=jnp.float32
    )
    allowed = (
        (query_label[:, None] == key_label[None, :])
        & (key_rank[None, :] < query_rank[:, None])
        & (key_label[None, :] >= 0)
    )
    return jnp.max(jnp.where(allowed, scores, -1.0), axis=1)


def per_device(embedding, cluster, member_order):
    normed = normalize(embedding)
    owners = lax.axis_size("dp")
    row_count = normed.shape[0]
    feature = normed.shape[1]
    capacity = max(2, 2 * row_count // owners)
    target = slot_index(cluster % owners, owners, capacity)
    packed, labels, ranks = pack_rows(normed, cluster, member_order, target, owners, capacity)
    arrived_rows, arrived_label, arrived_rank = (
        lax.all_to_all(packed, "dp", split_axis=0, concat_axis=0, tiled=True),
        lax.all_to_all(labels, "dp", split_axis=0, concat_axis=0, tiled=True),
        lax.all_to_all(ranks, "dp", split_axis=0, concat_axis=0, tiled=True),
    )
    queries = arrived_rows.reshape(-1, feature)
    query_label = arrived_label.reshape(-1)
    query_rank = arrived_rank.reshape(-1)
    start_best = jnp.full((queries.shape[0],), -1.0, jnp.float32)
    nearest = jnp.maximum(
        start_best,
        best_earlier(
            queries,
            query_label,
            query_rank,
            lax.all_gather(queries, "helper", axis=0, tiled=True),
            lax.all_gather(query_label, "helper", axis=0, tiled=True),
            lax.all_gather(query_rank, "helper", axis=0, tiled=True),
        ),
    )
    returned = lax.all_to_all(
        nearest.reshape(owners, capacity), "dp", split_axis=0, concat_axis=0, tiled=True
    )
    return returned.reshape(-1)[target]


def solution(mesh):
    in_specs = (P(("dp", "helper"), None), P(("dp", "helper")), P(("dp", "helper")))
    out_specs = P(("dp", "helper"))
    return jax.shard_map(
        per_device, mesh=mesh, in_specs=in_specs, out_specs=out_specs, check_vma=False
    )
```

profile of v0, /device:TPU:1, one launch (start us, length us, event | category | flops | bytes accessed | tf_op | source)
XLA Modules:
  0.0 169.2 jit_solution(12753068158171934671)
XLA Ops:
  6.5 0.0 copy-start.2
  6.5 0.0 copy-start.1
  6.5 0.0 all-gather.4.cloned.1.call-start
  6.5 0.8 fusion.18
  7.3 0.7 add_select_fusion
  8.0 1.4 fusion
  9.4 0.1 copy.6
  9.5 0.2 fusion.6
  9.7 0.1 broadcast_add_fusion
  9.8 0.2 fusion.9
  10.0 0.0 copy-done.2
  10.1 0.0 copy-done.1
  10.1 3.5 %scatter_custom_fusion.2 = bf16[768,1024]{1,0:T(8,128)(2,1)} fusion(s32[384]{0:T(512)S(1)} %compare_select_fusion, bf16[384,1024]{1,0:T(8,128)(2,1)S(1)} %copy-done.1, f32[384]{0:T(512)S(1)} %add_rsqrt_fusion, bf16[]{:T(256)} %constant.20.clone.1), kind=kCustom, calls=%fused_computation.9 | custom fusion | flops 1179648 | bytes 2361346 | tf_op jit(solution)/shard_map/scatter | solution.py:24
  13.5 2.5 %reshape.72 = bf16[128,6,1024]{2,1,0:T(8,128)(2,1)S(1)} reshape(bf16[768,1024]{1,0:T(8,128)(2,1)} %scatter_custom_fusion.2) | data formatting | bytes 3145728 | tf_op jit(solution)/shard_map/reshape | solution.py:28
  16.0 68.9 %all_to_all.29 = bf16[128,6,1024]{2,1,0:T(8,128)(2,1)} all-to-all(bf16[128,6,1024]{2,1,0:T(8,128)(2,1)S(1)} %reshape.72), channel_id=1, replica_groups=mesh['dp'=128,'helper'=2] {'dp'}, dimensions={0} | all-to-all | bytes 3145728 | tf_op jit(solution)/shard_map/all_to_all | solution.py:55
  85.0 3.7 %reshape.73 = bf16[768,1024]{1,0:T(8,128)(2,1)} reshape(bf16[128,6,1024]{2,1,0:T(8,128)(2,1)} %all_to_all.29) | data formatting | bytes 3145728 | tf_op jit(solution)/shard_map/reshape | solution.py:59
  88.7 0.0 copy-start
  88.7 0.0 all-gather.4.cloned.1.call-update
  88.7 2.9 %scatter_custom_fusion = s32[768]{0:T(1024)S(1)} fusion(s32[384]{0:T(512)S(1)} %compare_select_fusion, s32[384]{0:T(512)S(1)} %copy-done.2, s32[]{:T(128)} %constant.11.clone.1), kind=kCustom, calls=%fused_computation.33 | custom fusion | bytes 3076 | tf_op jit(solution)/shard_map/scatter | solution.py:25
  91.6 0.8 all_to_all.19
  92.4 6.1 %all-to-all-start = ((s32[128,1,6]{2,1,0:T(1,128)}), s32[128,1,6]{2,1,0:T(1,128)S(1)}, u32[]{:S(2)}, u32[]{:S(2)}) async-start(s32[128,1,6]{2,1,0:T(1,128)} %bitcast.4), calls=%async_computation | async-start | bytes 131072 | tf_op jit(solution)/shard_map/all_to_all | solution.py:56
  98.5 3.1 %scatter_custom_fusion.1 = s32[768]{0:T(1024)S(1)} fusion(s32[384]{0:T(512)S(1)} %compare_select_fusion, s32[384]{0:T(512)} %param.5, s32[]{:T(128)} %constant.12.clone.1), kind=kCustom, calls=%fused_computation.31 | custom fusion | bytes 3584 | tf_op jit(solution)/shard_map/scatter | solution.py:26
  101.6 0.8 all_to_all.21
  102.4 6.7 %all-to-all-done = s32[128,1,6]{2,1,0:T(1,128)S(1)} async-done(((s32[128,1,6]{2,1,0:T(1,128)}), s32[128,1,6]{2,1,0:T(1,128)S(1)}, u32[]{:S(2)}, u32[]{:S(2)}) %all-to-all-start) | async-done | bytes 3104 | tf_op jit(solution)/shard_map/all_to_all | solution.py:56
  109.1 6.5 %all-to-all-start.1 = ((s32[128,1,6]{2,1,0:T(1,128)}), s32[128,1,6]{2,1,0:T(1,128)S(1)}, u32[]{:S(2)}, u32[]{:S(2)}) async-start(s32[128,1,6]{2,1,0:T(1,128)} %bitcast.5), calls=%async_computation.1 | async-start | bytes 131072 | tf_op jit(solution)/shard_map/all_to_all | solution.py:57
  115.6 0.1 reshape.111
  115.8 5.0 %all-gather = s32[2,1,768]{2,1,0:T(1,128)S(1)} all-gather(s32[1,1,768]{2,1,0:T(1,128)S(1)} %reshape.111), channel_id=1, replica_groups=mesh['dp'=128,'helper'=2] {'helper'}, dimensions={0}, use_global_device_ids=true | all-gather | bytes 9216 | tf_op jit(solution)/shard_map/all_gather | solution.py:70
  120.8 5.4 %all-to-all-done.1 = s32[128,1,6]{2,1,0:T(1,128)S(1)} async-done(((s32[128,1,6]{2,1,0:T(1,128)}), s32[128,1,6]{2,1,0:T(1,128)S(1)}, u32[]{:S(2)}, u32[]{:S(2)}) %all-to-all-start.1) | async-done | bytes 3104 | tf_op jit(solution)/shard_map/all_to_all | solution.py:57
  126.2 0.1 reshape.71
  126.3 0.5 broadcast.72
  126.8 0.8 reduce.15
  127.7 0.1 reshape.113
  127.8 0.8 reduce.16
  128.6 0.1 eq.47
  128.8 6.1 %all-gather.1 = s32[2,1,768]{2,1,0:T(1,128)S(1)} all-gather(s32[1,1,768]{2,1,0:T(1,128)S(1)} %reshape.113), channel_id=1, replica_groups=mesh['dp'=128,'helper'=2] {'helper'}, dimensions={0}, use_global_device_ids=true | all-gather | bytes 9216 | tf_op jit(solution)/shard_map/all_gather | solution.py:71
  134.9 0.0 all-gather.4.cloned.1.call-done
  135.0 0.0 copy-done
  135.0 5.4 %select_reduce_fusion = f32[768]{0:T(1024)S(1)} fusion(bf16[768,1024]{1,0:T(8,128)(2,1)S(1)} %copy-done, bf16[1536,1024]{1,0:T(8,128)(2,1)} %all-gather.4.cloned.1.call-done, s32[1536]{0:T(1024)S(1)} %reshape.114, s32[1536]{0:T(1024)S(1)} %reshape.112, s32[768]{0:T(1024)S(1)} %reshape.71, s32[768]{0:T(1024)S(1)} %eq.47, ...), kind=kOutput, calls=%fused_computation.4 | convolution fusion | flops 2422996224 | bytes 4741632 | tf_op jit(solution)/shard_map/dot_general | solution.py:35
  140.4 0.8 max_broadcast_in_dim.15
  141.2 6.2 %all-to-all-start.3 = ((f32[128,1,6]{2,1,0:T(1,128)}), f32[128,1,6]{2,1,0:T(1,128)S(1)}, u32[]{:S(2)}, u32[]{:S(2)}) async-start(f32[128,1,6]{2,1,0:T(1,128)} %bitcast.6), calls=%async_computation.3 | async-start | bytes 131072 | tf_op jit(solution)/shard_map/all_to_all | solution.py:74
  147.4 10.5 %all-to-all-done.3 = f32[128,1,6]{2,1,0:T(1,128)S(1)} async-done(((f32[128,1,6]{2,1,0:T(1,128)}), f32[128,1,6]{2,1,0:T(1,128)S(1)}, u32[]{:S(2)}, u32[]{:S(2)}) %all-to-all-start.3) | async-done | bytes 3104 | tf_op jit(solution)/shard_map/all_to_all | solution.py:74
  157.9 0.5 broadcast.74
  158.4 0.8 reduce.17
  159.3 0.1 reshape.74
  159.4 3.0 %gather_fusion = f32[384]{0:T(512)} fusion(f32[768]{0:T(1024)S(1)} %reshape.74, s32[1024]{0:T(1024)S(1)} %pad_clamp_fusion), kind=kCustom, calls=%fused_computation | custom fusion | bytes 4608 | tf_op jit(solution)/shard_map/gather | solution.py:77
  (12 shorter events, 0.2 us)
Async XLA Ops:
  6.5 3.5 %copy-start.2 = (s32[384]{0:T(512)S(1)}, s32[384]{0:T(512)}, u32[]{:S(2)}) copy-start(s32[384]{0:T(512)} %param.4) | copy-start | bytes 4612
  6.5 3.5 %copy-start.1 = (bf16[384,1024]{1,0:T(8,128)(2,1)S(1)}, bf16[384,1024]{1,0:T(8,128)(2,1)}, u32[]{:S(2)}) copy-start(bf16[384,1024]{1,0:T(8,128)(2,1)} %param.3) | copy-start | bytes 2359300
  6.5 128.4 %all-gather.4.cloned.1.call-start = ((), (), s32[]{:S(2)}) async-start(), calls=%async_computation.4 | async-start | bytes 4718592 | tf_op jit(solution)/shard_map/all_gather | solution.py:69
  88.7 46.3 %copy-start = (bf16[768,1024]{1,0:T(8,128)(2,1)S(1)}, bf16[768,1024]{1,0:T(8,128)(2,1)}, u32[]{:S(2)}) copy-start(bf16[768,1024]{1,0:T(8,128)(2,1)} %reshape.73) | copy-start | bytes 4718596
  92.4 16.7 %all-to-all-start = ((s32[128,1,6]{2,1,0:T(1,128)}), s32[128,1,6]{2,1,0:T(1,128)S(1)}, u32[]{:S(2)}, u32[]{:S(2)}) async-start(s32[128,1,6]{2,1,0:T(1,128)} %bitcast.4), calls=%async_computation | async-start | bytes 131072 | tf_op jit(solution)/shard_map/all_to_all | solution.py:56
  109.1 17.1 %all-to-all-start.1 = ((s32[128,1,6]{2,1,0:T(1,128)}), s32[128,1,6]{2,1,0:T(1,128)S(1)}, u32[]{:S(2)}, u32[]{:S(2)}) async-start(s32[128,1,6]{2,1,0:T(1,128)} %bitcast.5), calls=%async_computation.1 | async-start | bytes 131072 | tf_op jit(solution)/shard_map/all_to_all | solution.py:57
  141.2 16.7 %all-to-all-start.3 = ((f32[128,1,6]{2,1,0:T(1,128)}), f32[128,1,6]{2,1,0:T(1,128)S(1)}, u32[]{:S(2)}, u32[]{:S(2)}) async-start(f32[128,1,6]{2,1,0:T(1,128)} %bitcast.6), calls=%async_computation.3 | async-start | bytes 131072 | tf_op jit(solution)/shard_map/all_to_all | solution.py:74
Sparse Core Ops, SparseCore 0:
  88.8 12.4 all-gather.3
where the time goes:
time: 170 us; the launch traced here: 169 us
  blocking collectives  80.1 us (47%)
  waiting for transfers between devices  22.7 us (13%)
  local copies, waits for them, and re-layouts  19.3 us (11%)
  starting transfers between devices  18.9 us (11%)
  between operations  13.6 us (8%)
  other arithmetic  9.31 us (5%)
  matrix products  5.43 us (3%)
    all_to_all x1, blocking collectives, per_device(): lax.all_to_all(packed, 'dp', split_axis=0, concat_axis=0, tiled=True)  68.9 us
    all_to_all x1, waiting for transfers between devices, per_device(): lax.all_to_all(nearest.reshape(owners, capacity), 'dp', split_axis=0, con...  10.5 us
    all_to_all x1, waiting for transfers between devices, per_device(): lax.all_to_all(labels, 'dp', split_axis=0, concat_axis=0, tiled=True)  6.72 us
    all_to_all x1, starting transfers between devices, per_device(): lax.all_to_all(ranks, 'dp', split_axis=0, concat_axis=0, tiled=True)  6.54 us
    all_to_all x1, starting transfers between devices, per_device(): lax.all_to_all(nearest.reshape(owners, capacity), 'dp', split_axis=0, con...  6.17 us
    all_to_all x1, starting transfers between devices, per_device(): lax.all_to_all(labels, 'dp', split_axis=0, concat_axis=0, tiled=True)  6.15 us
    all_gather x1, blocking collectives, per_device(): lax.all_gather(query_rank, 'helper', axis=0, tiled=True)  6.14 us
    dot_general x1, matrix products, best_earlier(): lax.dot_general(queries, key_rows, (((1,), (1,)), ((), ())), preferred_el...  5.43 us
  transfers between devices with their start and end apart: 4, of which 3 were waited for; matrix products, arithmetic and copies ran while one was open for 5% of the time, Pallas kernels for 0%

commit v1 on v0

v1 whole, which is shorter than its diff:
```python
import functools

import jax
import jax.numpy as jnp
from jax import lax
from jax.experimental import pallas as pl
from jax.experimental.pallas import tpu as pltpu
from jax.sharding import PartitionSpec as P

LANES = 128
META = 8
CLASS = 1 << 17
VMEM_LIMIT = 48 << 20


def routing(cluster, owners):
    count = cluster.shape[1]
    owner = lax.rem(cluster, owners)
    member = lax.broadcasted_iota(jnp.int32, (owners, count), 0) == owner
    before = lax.broadcasted_iota(jnp.int32, (count, count), 0) < lax.broadcasted_iota(
        jnp.int32, (count, count), 1
    )
    ones = member.astype(jnp.bfloat16)
    earlier = jnp.dot(ones, before.astype(jnp.bfloat16), preferred_element_type=jnp.float32)
    slot = jnp.sum(jnp.where(member, earlier, 0.0), axis=0, keepdims=True).astype(jnp.int32)
    return member, slot


def pack_kernel(owners, cap, cluster_ref, order_ref, x_ref, out_ref, wide):
    chunks = x_ref.shape[1] // LANES
    block = cap * chunks + META
    cluster = cluster_ref[...]
    order = order_ref[...]
    member, slot = routing(cluster, owners)
    values = x_ref[...].astype(jnp.float32)
    scale = lax.rsqrt(jnp.sum(values * values, axis=1, keepdims=True) + 1e-06)
    normed = (values * scale).astype(jnp.bfloat16)
    for s in range(cap):
        pick = (member & (slot == s)).astype(jnp.bfloat16)
        rows = jnp.dot(pick, normed, preferred_element_type=jnp.float32)
        for j in range(chunks):
            wide[pl.ds(s * chunks + j, owners, stride=block), :] = rows[
                :, j * LANES : (j + 1) * LANES
            ]
    ones = member.astype(jnp.bfloat16)
    place = lax.broadcasted_iota(jnp.int32, (LANES, cluster.shape[1]), 0) == slot
    digits = (order & 255, (order >> 8) & 255, (order >> 16) + 2 * lax.div(cluster, owners) + 8)
    for r in range(META):
        if r < len(digits):
            spread = jnp.where(place, digits[r].astype(jnp.float32), 0.0).astype(jnp.bfloat16)
            rows = lax.dot_general(
                ones, spread, (((1,), (1,)), ((), ())), preferred_element_type=jnp.float32
            )
        else:
            rows = jnp.zeros((owners, LANES), jnp.float32)
        wide[pl.ds(cap * chunks + r, owners, stride=block), :] = rows
    out_ref[...] = wide[...].astype(jnp.bfloat16)


def unpack(sources, cap, block_ref, wide, rows_ref):
    chunks = rows_ref.shape[1] // LANES
    block = cap * chunks + META
    wide[...] = block_ref[...].astype(jnp.float32)
    for s in range(cap):
        for j in range(chunks):
            rows_ref[s * sources : (s + 1) * sources, j * LANES : (j + 1) * LANES] = wide[
                pl.ds(s * chunks + j, sources, stride=block), :
            ].astype(jnp.bfloat16)
    digit = [wide[pl.ds(cap * chunks + r, sources, stride=block), :] for r in range(3)]
    return (digit[0] + 256.0 * digit[1] + 65536.0 * digit[2]).astype(jnp.int32)


def best_of(sources, cap, keys_ref, key_value, queries_ref, query_value, best_ref):
    turned = query_value.T
    for q in range(cap):
        mine = turned[q : q + 1, :]
        floor = mine & ~(CLASS - 1)
        best = best_ref[q : q + 1, :]
        queries = queries_ref[q * sources : (q + 1) * sources, :]
        for k in range(cap):
            scores = lax.dot_general(
                keys_ref[k * sources : (k + 1) * sources, :],
                queries,
                (((1,), (1,)), ((), ())),
                preferred_element_type=jnp.float32,
            )
            theirs = key_value[:, k : k + 1]
            allowed = (theirs >= floor) & (theirs < mine)
            best = jnp.maximum(
                best, jnp.max(jnp.where(allowed, scores, -1.0), axis=0, keepdims=True)
            )
        best_ref[q : q + 1, :] = best


def own_kernel(sources, cap, block_ref, rows_ref, value_ref, best_ref, wide):
    value = unpack(sources, cap, block_ref, wide, rows_ref)
    value_ref[...] = value
    best_ref[...] = jnp.full(best_ref.shape, -1.0, jnp.float32)
    best_of(sources, cap, rows_ref, value, rows_ref, value, best_ref)


def other_kernel(
    sources, cap, block_ref, own_ref, own_value_ref, own_best_ref, out_ref, wide, rows, best
):
    value = unpack(sources, cap, block_ref, wide, rows)
    best[...] = jnp.full(best.shape, -1.0, jnp.float32)
    best[: own_best_ref.shape[0], :] = own_best_ref[...]
    best_of(sources, cap, rows, value, own_ref, own_value_ref[...], best)
    out_ref[...] = best[...].T


def pick_kernel(owners, cap, cluster_ref, result_ref, out_ref):
    member, slot = routing(cluster_ref[...], owners)
    result = result_ref[...]
    found = jnp.full(slot.shape, -1.0, jnp.float32)
    for s in range(cap):
        here = jnp.max(
            jnp.where(member, result[:, s : s + 1], -2.0), axis=0, keepdims=True
        )
        found = jnp.where(slot == s, here, found)
    out_ref[...] = found


def call(kernel, out_shape, scratch=()):
    return pl.pallas_call(
        kernel,
        out_shape=out_shape,
        scratch_shapes=list(scratch),
        compiler_params=pltpu.CompilerParams(vmem_limit_bytes=VMEM_LIMIT),
    )


def per_device(embedding, cluster, member_order):
    owners = lax.axis_size("dp")
    count, feature = embedding.shape
    cap = max(2, 2 * count // owners)
    block = cap * feature // LANES + META
    cluster = cluster.reshape(1, count)
    order = member_order.reshape(1, count)
    shape = jax.ShapeDtypeStruct
    wide = pltpu.VMEM((owners * block, LANES), jnp.float32)
    packed = call(
        functools.partial(pack_kernel, owners, cap),
        shape((owners * block, LANES), jnp.bfloat16),
        [wide],
    )(cluster, order, embedding)
    arrived = lax.all_to_all(
        packed.reshape(owners, block, LANES), "dp", split_axis=0, concat_axis=0, tiled=True
    ).reshape(owners * block, LANES)
    other = lax.ppermute(arrived, "helper", [(0, 1), (1, 0)])
    rows, value, best = call(
        functools.partial(own_kernel, owners, cap),
        (
            shape((owners * cap, feature), jnp.bfloat16),
            shape((owners, LANES), jnp.int32),
            shape((8, owners), jnp.float32),
        ),
        [wide],
    )(arrived)
    nearest = call(
        functools.partial(other_kernel, owners, cap),
        shape((owners, LANES), jnp.float32),
        [
            wide,
            pltpu.VMEM((owners * cap, feature), jnp.bfloat16),
            pltpu.VMEM((LANES, owners), jnp.float32),
        ],
    )(other, rows, value, best)
    returned = lax.all_to_all(
        nearest.reshape(owners, 1, LANES), "dp", split_axis=0, concat_axis=0, tiled=True
    ).reshape(owners, LANES)
    found = call(
        functools.partial(pick_kernel, owners, cap), shape((1, count), jnp.float32)
    )(cluster, returned)
    return found.reshape(count)


def solution(mesh):
    in_specs = (P(("dp", "helper"), None), P(("dp", "helper")), P(("dp", "helper")))
    out_specs = P(("dp", "helper"))
    return jax.shard_map(
        per_device, mesh=mesh, in_specs=in_specs, out_specs=out_specs, check_vma=False
    )
```

time: 170 us -> 93.9 us (0.55)
  waiting for transfers between devices: 22.7 us -> 0.24 us
  local copies, waits for them, and re-layouts: 19.3 us -> 2.5 us
  starting transfers between devices: 18.9 us -> 2.59 us
  between operations: 13.6 us -> 0.03 us
  other arithmetic: 9.31 us -> 0.6 us
  Pallas kernels: 0 us -> 8.37 us
  matrix products: 5.43 us -> 0 us
    all_to_all x3 -> x0, waiting for transfers between devices: 22.6 us -> none  [the longest x1 10.5 us: per_device(): lax.all_to_all(nearest.reshape(owners, capacity), 'dp', split_axis=0, con...]
    all_to_all x3 -> x0, starting transfers between devices: 18.9 us -> none  [the longest x1 6.54 us: per_device(): lax.all_to_all(ranks, 'dp', split_axis=0, concat_axis=0, tiled=True)]
    all_gather x2 -> x0, blocking collectives: 11.1 us -> none  [the longest x1 6.14 us: per_device(): lax.all_gather(query_rank, 'helper', axis=0, tiled=True)]
    all_to_all x1 -> x2, blocking collectives: 68.9 us -> 79.4 us  [the longest x1 63.3 us: per_device(): lax.all_to_all(packed.reshape(owners, block, LANES), 'dp', split_axis=0,...]
    pallas_call x0 -> x4, Pallas kernels: none -> 8.37 us  [the longest x1 3.26 us: per_device(): call(functools.partial(other_kernel, owners, cap), shape((owners, LANES),...]
    scatter x2 -> x0, local copies, waits for them, and re-layouts: 6 us -> none  [the longest x1 3.08 us: pack_rows(): ranks = jnp.zeros((slot_total,), jnp.int32).at[target].set(member_order)]
    dot_general x1 -> x0, matrix products: 5.43 us -> none  [best_earlier(): lax.dot_general(queries, key_rows, (((1,), (1,)), ((), ())), preferred_el...]
    reshape x4 -> x2, local copies, waits for them, and re-layouts: 6.44 us -> 1.37 us  [the longest x1 0.68 us: per_device(): cluster = cluster.reshape(1, count)]
  transfers between devices with their start and end apart: 4 -> 1, of which waited for: 3 -> 1; matrix products, arithmetic and copies ran while one was open for 5% -> 0% of each run, Pallas kernels for 0% -> 3%
where the time goes in v1:
time: 93.9 us; the launch traced here: 93.7 us
  blocking collectives  79.4 us (85%)
  Pallas kernels  8.37 us (9%)
  starting transfers between devices  2.59 us (3%)
  local copies, waits for them, and re-layouts  2.5 us (3%)
    all_to_all x1, blocking collectives, per_device(): lax.all_to_all(packed.reshape(owners, block, LANES), 'dp', split_axis=0,...  63.3 us
    all_to_all x1, blocking collectives, per_device(): lax.all_to_all(nearest.reshape(owners, 1, LANES), 'dp', split_axis=0, con...  16.1 us
    pallas_call x1, Pallas kernels, per_device(): call(functools.partial(other_kernel, owners, cap), shape((owners, LANES),...  3.26 us
    pallas_call x1, Pallas kernels, per_device(): call(functools.partial(own_kernel, owners, cap), (shape((owners * cap, fe...  3.17 us
    ppermute x1, starting transfers between devices, per_device(): other = lax.ppermute(arrived, 'helper', [(0, 1), (1, 0)])  2.59 us
  transfers between devices with their start and end apart: 1, of which 1 were waited for; matrix products, arithmetic and copies ran while one was open for 0% of the time, Pallas kernels for 3%

profile of v1, /device:TPU:1, one launch (start us, length us, event | category | flops | bytes accessed | tf_op | source)
XLA Modules:
  0.0 93.7 jit_solution(9267375565651862509)
XLA Ops:
  0.0 0.7 reshape.21.cluster_ref
  0.7 0.7 reshape.22.order_ref
  1.4 0.0 copy-start
  1.4 1.1 %copy-done = bf16[384,1024]{1,0:T(8,128)(2,1)S(1)} copy-done((bf16[384,1024]{1,0:T(8,128)(2,1)S(1)}, bf16[384,1024]{1,0:T(8,128)(2,1)}, u32[]{:S(2)}) %copy-start) | copy-done | bytes 786456
  2.5 1.7 %shard_map.37 = bf16[7168,128]{1,0:T(8,128)(2,1)S(1)} custom-call(s32[1,384]{1,0:T(1,128)S(1)} %reshape.21.cluster_ref, s32[1,384]{1,0:T(1,128)S(1)} %reshape.22.order_ref, bf16[384,1024]{1,0:T(8,128)(2,1)S(1)} %copy-done), custom_call_target="tpu_custom_call" | custom-call | tf_op jit(solution)/shard_map/pallas_call | solution.py:142
  4.2 63.3 %all_to_all.10 = bf16[128,56,128]{2,1,0:T(8,128)(2,1)S(1)} all-to-all(bf16[128,56,128]{2,1,0:T(8,128)(2,1)S(1)} %bitcast.8), channel_id=1, replica_groups=mesh['dp'=128,'helper'=2] {'dp'}, dimensions={0} | all-to-all | bytes 3670016 | tf_op jit(solution)/shard_map/all_to_all | solution.py:147
  67.5 2.6 %collective-permute-start = (bf16[7168,128]{1,0:T(8,128)(2,1)S(1)}, bf16[7168,128]{1,0:T(8,128)(2,1)S(1)}, u32[]{:S(2)}, u32[]{:S(2)}) collective-permute-start(bf16[7168,128]{1,0:T(8,128)(2,1)S(1)} %bitcast.6), channel_id=1, source_target_pairs={{0,1},{1,0},{2,3},{3,2},{4,5},{5,4},{6,7},{7,6},{8,9},{9,8},{10,11... | collective-permute-start | bytes 5505032 | tf_op jit(solution)/shard_map/ppermute | solution.py:150
  70.1 3.2 %shard_map.38 = (bf16[768,1024]{1,0:T(8,128)(2,1)S(1)}, s32[128,128]{1,0:T(8,128)S(1)}, f32[8,128]{1,0:T(8,128)S(1)}) custom-call(bf16[7168,128]{1,0:T(8,128)(2,1)S(1)} %bitcast.7), custom_call_target="tpu_custom_call" | custom-call | tf_op jit(solution)/shard_map/pallas_call | solution.py:151
  73.3 0.2 collective-permute-done.block_ref
  73.5 3.3 %shard_map.39 = f32[128,128]{1,0:T(8,128)S(1)} custom-call(bf16[7168,128]{1,0:T(8,128)(2,1)S(1)} %collective-permute-done.block_ref, bf16[768,1024]{1,0:T(8,128)(2,1)S(1)} %get-tuple-element.8.own_ref, s32[128,128]{1,0:T(8,128)S(1)} %get-tuple-element.9.own_value_ref, f32[8,128]{1,0:T(8,128)S(1)} %get-tuple-element.10.own_best_ref), custom_call_target="tpu_custom_call" | custom-call | tf_op jit(solution)/shard_map/pallas_call | solution.py:160
  76.8 16.1 %all_to_all.11 = f32[128,1,128]{2,1,0:T(1,128)S(1)} all-to-all(f32[128,1,128]{2,1,0:T(1,128)S(1)} %bitcast.9), channel_id=1, replica_groups=mesh['dp'=128,'helper'=2] {'dp'}, dimensions={0} | all-to-all | bytes 131072 | tf_op jit(solution)/shard_map/all_to_all | solution.py:169
  92.8 0.2 shard_map.40
  93.1 0.6 reduce
Async XLA Ops:
  1.4 1.1 %copy-start = (bf16[384,1024]{1,0:T(8,128)(2,1)S(1)}, bf16[384,1024]{1,0:T(8,128)(2,1)}, u32[]{:S(2)}) copy-start(bf16[384,1024]{1,0:T(8,128)(2,1)} %x_ref.1) | copy-start | bytes 2359300
  67.5 6.0 %collective-permute-start = (bf16[7168,128]{1,0:T(8,128)(2,1)S(1)}, bf16[7168,128]{1,0:T(8,128)(2,1)S(1)}, u32[]{:S(2)}, u32[]{:S(2)}) collective-permute-start(bf16[7168,128]{1,0:T(8,128)(2,1)S(1)} %bitcast.6), channel_id=1, source_target_pairs={{0,1},{1,0},{2,3},{3,2},{4,5},{5,4},{6,7},{7,6},{8,9},{9,8},{10,11... | collective-permute-start | bytes 5505032 | tf_op jit(solution)/shard_map/ppermute | solution.py:150

commit v2 on v1

--- a/solution.py
+++ b/solution.py
@@ -8,7 +8,8 @@
 from jax.sharding import PartitionSpec as P
 
 LANES = 128
-META = 8
+META = 2
+SIDE = 8
 CLASS = 1 << 17
 VMEM_LIMIT = 48 << 20
 
@@ -26,12 +27,40 @@
     return member, slot
 
 
-def pack_kernel(owners, cap, cluster_ref, order_ref, x_ref, out_ref, wide):
-    chunks = x_ref.shape[1] // LANES
+def pack_kernel(
+    owners, cap, cluster_hbm, order_hbm, x_hbm, out_ref, cluster_ref, order_ref, x_ref, wide, arrived
+):
+    given = (cluster_hbm, order_hbm, x_hbm)
+    fetch = [
+        pltpu.make_async_copy(source, target, arrived.at[i])
+        for i, (source, target) in enumerate(zip(given, (cluster_ref, order_ref, x_ref)))
+    ]
+    for copy in fetch:
+        copy.start()
+    fetch[0].wait()
+    fetch[1].wait()
+    count, feature = x_ref.shape
+    chunks = feature // LANES
     block = cap * chunks + META
-    cluster = cluster_ref[...]
-    order = order_ref[...]
+    cluster = cluster_ref[...].reshape(1, count)
+    order = order_ref[...].reshape(1, count)
     member, slot = routing(cluster, owners)
+    ones = member.astype(jnp.bfloat16)
+    lane = lax.broadcasted_iota(jnp.int32, (LANES, count), 0)
+    low, middle = order & 255, (order >> 8) & 255
+    high = (order >> 16) + 2 * lax.div(cluster, owners) + 8
+    spread = (
+        jnp.where(lane == slot, low, jnp.where(lane == slot + SIDE, middle, 0)),
+        jnp.where(lane == slot, high, 0),
+    )
+    for r in range(META):
+        wide[pl.ds(cap * chunks + r, owners, stride=block), :] = lax.dot_general(
+            ones,
+            spread[r].astype(jnp.float32).astype(jnp.bfloat16),
+            (((1,), (1,)), ((), ())),
+            preferred_element_type=jnp.float32,
+        )
+    fetch[2].wait()
     values = x_ref[...].astype(jnp.float32)
     scale = lax.rsqrt(jnp.sum(values * values, axis=1, keepdims=True) + 1e-06)
     normed = (values * scale).astype(jnp.bfloat16)
@@ -42,18 +71,6 @@
             wide[pl.ds(s * chunks + j, owners, stride=block), :] = rows[
                 :, j * LANES : (j + 1) * LANES
             ]
-    ones = member.astype(jnp.bfloat16)
-    place = lax.broadcasted_iota(jnp.int32, (LANES, cluster.shape[1]), 0) == slot
-    digits = (order & 255, (order >> 8) & 255, (order >> 16) + 2 * lax.div(cluster, owners) + 8)
-    for r in range(META):
-        if r < len(digits):
-            spread = jnp.where(place, digits[r].astype(jnp.float32), 0.0).astype(jnp.bfloat16)
-            rows = lax.dot_general(
-                ones, spread, (((1,), (1,)), ((), ())), preferred_element_type=jnp.float32
-            )
-        else:
-            rows = jnp.zeros((owners, LANES), jnp.float32)
-        wide[pl.ds(cap * chunks + r, owners, stride=block), :] = rows
     out_ref[...] = wide[...].astype(jnp.bfloat16)
 
 
@@ -66,30 +83,35 @@
             rows_ref[s * sources : (s + 1) * sources, j * LANES : (j + 1) * LANES] = wide[
                 pl.ds(s * chunks + j, sources, stride=block), :
             ].astype(jnp.bfloat16)
-    digit = [wide[pl.ds(cap * chunks + r, sources, stride=block), :] for r in range(3)]
-    return (digit[0] + 256.0 * digit[1] + 65536.0 * digit[2]).astype(jnp.int32)
+    digit = [wide[pl.ds(cap * chunks + r, sources, stride=block), :] for r in range(META)]
+    middle = pltpu.roll(digit[0], LANES - SIDE, 1)
+    return (digit[0] + 256.0 * middle + 65536.0 * digit[1]).astype(jnp.int32)
 
 
 def best_of(sources, cap, keys_ref, key_value, queries_ref, query_value, best_ref):
     turned = query_value.T
-    for q in range(cap):
-        mine = turned[q : q + 1, :]
-        floor = mine & ~(CLASS - 1)
-        best = best_ref[q : q + 1, :]
-        queries = queries_ref[q * sources : (q + 1) * sources, :]
-        for k in range(cap):
+    step = 2 if cap % 2 == 0 else 1
+    for q in range(0, cap, step):
+        queries = queries_ref[q * sources : (q + step) * sources, :]
+        best = [best_ref[q + i : q + i + 1, :] for i in range(step)]
+        for k in range(0, cap, step):
             scores = lax.dot_general(
-                keys_ref[k * sources : (k + 1) * sources, :],
+                keys_ref[k * sources : (k + step) * sources, :],
                 queries,
                 (((1,), (1,)), ((), ())),
                 preferred_element_type=jnp.float32,
             )
-            theirs = key_value[:, k : k + 1]
-            allowed = (theirs >= floor) & (theirs < mine)
-            best = jnp.maximum(
-                best, jnp.max(jnp.where(allowed, scores, -1.0), axis=0, keepdims=True)
-            )
-        best_ref[q : q + 1, :] = best
+            for i in range(step):
+                mine = turned[q + i : q + i + 1, :]
+                floor = mine & ~(CLASS - 1)
+                for m in range(step):
+                    theirs = key_value[:, k + m : k + m + 1]
+                    allowed = (theirs >= floor) & (theirs < mine)
+                    part = scores[m * sources : (m + 1) * sources, i * sources : (i + 1) * sources]
+                    top = jnp.max(jnp.where(allowed, part, -1.0), axis=0, keepdims=True)
+                    best[i] = jnp.maximum(best[i], top)
+        for i in range(step):
+            best_ref[q + i : q + i + 1, :] = best[i]
 
 
 def own_kernel(sources, cap, block_ref, rows_ref, value_ref, best_ref, wide):
@@ -110,7 +132,8 @@
 
 
 def pick_kernel(owners, cap, cluster_ref, result_ref, out_ref):
-    member, slot = routing(cluster_ref[...], owners)
+    count = cluster_ref.shape[0]
+    member, slot = routing(cluster_ref[...].reshape(1, count), owners)
     result = result_ref[...]
     found = jnp.full(slot.shape, -1.0, jnp.float32)
     for s in range(cap):
@@ -118,15 +141,16 @@
             jnp.where(member, result[:, s : s + 1], -2.0), axis=0, keepdims=True
         )
         found = jnp.where(slot == s, here, found)
-    out_ref[...] = found
-
-
-def call(kernel, out_shape, scratch=()):
+    out_ref[...] = found.reshape(count)
+
+
+def call(kernel, out_shape, scratch=(), in_specs=None):
     return pl.pallas_call(
         kernel,
         out_shape=out_shape,
         scratch_shapes=list(scratch),
         compiler_params=pltpu.CompilerParams(vmem_limit_bytes=VMEM_LIMIT),
+        **({} if in_specs is None else {"in_specs": in_specs}),
     )
 
 
@@ -135,17 +159,17 @@
     count, feature = embedding.shape
     cap = max(2, 2 * count // owners)
     block = cap * feature // LANES + META
-    cluster = cluster.reshape(1, count)
-    order = member_order.reshape(1, count)
     shape = jax.ShapeDtypeStruct
     wide = pltpu.VMEM((owners * block, LANES), jnp.float32)
     packed = call(
         functools.partial(pack_kernel, owners, cap),
         shape((owners * block, LANES), jnp.bfloat16),
-        [wide],
-    )(cluster, order, embedding)
+        [pltpu.VMEM(x.shape, x.dtype) for x in (cluster, member_order, embedding)]
+        + [wide, pltpu.SemaphoreType.DMA((3,))],
+        [pl.BlockSpec(memory_space=pltpu.HBM)] * 3,
+    )(cluster, member_order, embedding)
     arrived = lax.all_to_all(
-        packed.reshape(owners, block, LANES), "dp", split_axis=0, concat_axis=0, tiled=True
+        packed.reshape(owners, block // 2, 2, LANES), "dp", split_axis=0, concat_axis=0, tiled=True
     ).reshape(owners * block, LANES)
     other = lax.ppermute(arrived, "helper", [(0, 1), (1, 0)])
     rows, value, best = call(
@@ -169,10 +193,9 @@
     returned = lax.all_to_all(
         nearest.reshape(owners, 1, LANES), "dp", split_axis=0, concat_axis=0, tiled=True
     ).reshape(owners, LANES)
-    found = call(
-        functools.partial(pick_kernel, owners, cap), shape((1, count), jnp.float32)
-    )(cluster, returned)
-    return found.reshape(count)
+    return call(functools.partial(pick_kernel, owners, cap), shape((count,), jnp.float32))(
+        cluster, returned
+    )
 
 
 def solution(mesh):

time: 93.9 us -> 88.2 us (0.939)
  blocking collectives: 79.4 us -> 75.3 us
  Pallas kernels: 8.37 us -> 6.41 us
  waiting for transfers between devices: 0.24 us -> 1.28 us
    all_to_all x1, blocking collectives: 63.3 us -> 59.2 us  [per_device(): lax.all_to_all(packed.reshape(owners, block // 2, 2, LANES), 'dp', split_...]
    unnamed x2 -> x8, local copies, waits for them, and re-layouts: 1.13 us -> 2.5 us
    reshape x2 -> x0, local copies, waits for them, and re-layouts: 1.37 us -> none  [the longest x1 0.68 us: per_device(): cluster = cluster.reshape(1, count)]
    pallas_call x1, Pallas kernels: 3.26 us -> 1.92 us  [per_device(): call(functools.partial(other_kernel, owners, cap), shape((owners, LANES),...]
    pallas_call x1, Pallas kernels: 3.17 us -> 1.84 us  [per_device(): call(functools.partial(own_kernel, owners, cap), (shape((owners * cap, fe...]
    ppermute x1, waiting for transfers between devices: 0.24 us -> 1.28 us  [per_device(): other = lax.ppermute(arrived, 'helper', [(0, 1), (1, 0)])]
  transfers between devices with their start and end apart: 1 -> 1, of which waited for: 1 -> 1; matrix products, arithmetic and copies ran while one was open for 0% -> 0% of each run, Pallas kernels for 3% -> 2%
where the time goes in v2:
time: 88.2 us; the launch traced here: 88 us
  blocking collectives  75.3 us (85%)
  Pallas kernels  6.41 us (7%)
  local copies, waits for them, and re-layouts  2.5 us (3%)
  starting transfers between devices  2.45 us (3%)
  waiting for transfers between devices  1.28 us (1%)
    all_to_all x1, blocking collectives, per_device(): lax.all_to_all(packed.reshape(owners, block // 2, 2, LANES), 'dp', split_...  59.2 us
    all_to_all x1, blocking collectives, per_device(): lax.all_to_all(nearest.reshape(owners, 1, LANES), 'dp', split_axis=0, con...  16.1 us
    unnamed x8, local copies, waits for them, and re-layouts  2.5 us
    ppermute x1, starting transfers between devices, per_device(): other = lax.ppermute(arrived, 'helper', [(0, 1), (1, 0)])  2.45 us
    pallas_call x1, Pallas kernels, per_device(): call(functools.partial(other_kernel, owners, cap), shape((owners, LANES),...  1.92 us
    pallas_call x1, Pallas kernels, per_device(): call(functools.partial(pack_kernel, owners, cap), shape((owners * block,...  1.85 us
    pallas_call x1, Pallas kernels, per_device(): call(functools.partial(own_kernel, owners, cap), (shape((owners * cap, fe...  1.84 us
  transfers between devices with their start and end apart: 1, of which 1 were waited for; matrix products, arithmetic and copies ran while one was open for 0% of the time, Pallas kernels for 2%

profile of v2, /device:TPU:1, one launch (start us, length us, event | category | flops | bytes accessed | tf_op | source)
XLA Modules:
  0.0 88.0 jit_solution(4775722636816209559)
XLA Ops:
  0.0 0.0 copy-start
  0.0 1.1 %copy-done = bf16[384,1024]{1,0:T(8,128)(2,1)S(1)} copy-done((bf16[384,1024]{1,0:T(8,128)(2,1)S(1)}, bf16[384,1024]{1,0:T(8,128)(2,1)}, u32[]{:S(2)}) %copy-start) | copy-done | bytes 786456
  1.1 0.0 copy-start.1
  1.1 0.7 copy-done.1
  1.8 0.0 copy-start.3
  1.8 0.7 copy-done.3
  2.5 1.9 %shard_map.37 = bf16[6400,128]{1,0:T(8,128)(2,1)S(1)} custom-call(s32[384]{0:T(512)S(1)} %copy-done.1, s32[384]{0:T(512)S(1)} %copy-done.3, bf16[384,1024]{1,0:T(8,128)(2,1)S(1)} %copy-done), custom_call_target="tpu_custom_call" | custom-call | tf_op jit(solution)/shard_map/pallas_call | solution.py:164
  4.4 59.2 %all_to_all.10 = bf16[128,25,2,128]{3,2,1,0:T(2,128)(2,1)S(1)} all-to-all(bf16[128,25,2,128]{3,2,1,0:T(2,128)(2,1)S(1)} %bitcast.8), channel_id=1, replica_groups=mesh['dp'=128,'helper'=2] {'dp'}, dimensions={0} | all-to-all | bytes 3276800 | tf_op jit(solution)/shard_map/all_to_all | solution.py:171
  63.6 2.4 %collective-permute-start = (bf16[6400,128]{1,0:T(8,128)(2,1)S(1)}, bf16[6400,128]{1,0:T(8,128)(2,1)S(1)}, u32[]{:S(2)}, u32[]{:S(2)}) collective-permute-start(bf16[6400,128]{1,0:T(8,128)(2,1)S(1)} %bitcast.6), channel_id=1, source_target_pairs={{0,1},{1,0},{2,3},{3,2},{4,5},{5,4},{6,7},{7,6},{8,9},{9,8},{10,11... | collective-permute-start | bytes 4915208 | tf_op jit(solution)/shard_map/ppermute | solution.py:174
  66.0 1.8 %shard_map.38 = (bf16[768,1024]{1,0:T(8,128)(2,1)S(1)}, s32[128,128]{1,0:T(8,128)S(1)}, f32[8,128]{1,0:T(8,128)S(1)}) custom-call(bf16[6400,128]{1,0:T(8,128)(2,1)S(1)} %bitcast.7), custom_call_target="tpu_custom_call" | custom-call | tf_op jit(solution)/shard_map/pallas_call | solution.py:175
  67.9 1.3 %collective-permute-done.block_ref = bf16[6400,128]{1,0:T(8,128)(2,1)S(1)} collective-permute-done((bf16[6400,128]{1,0:T(8,128)(2,1)S(1)}, bf16[6400,128]{1,0:T(8,128)(2,1)S(1)}, u32[]{:S(2)}, u32[]{:S(2)}) %collective-permute-start) | collective-permute-done | bytes 1638432 | tf_op jit(solution)/shard_map/ppermute | solution.py:174
  69.1 0.0 copy-start.2
  69.1 1.9 %shard_map.39 = f32[128,128]{1,0:T(8,128)S(1)} custom-call(bf16[6400,128]{1,0:T(8,128)(2,1)S(1)} %collective-permute-done.block_ref, bf16[768,1024]{1,0:T(8,128)(2,1)S(1)} %get-tuple-element.8.own_ref, s32[128,128]{1,0:T(8,128)S(1)} %get-tuple-element.9.own_value_ref, f32[8,128]{1,0:T(8,128)S(1)} %get-tuple-element.10.own_best_ref), custom_call_target="tpu_custom_call" | custom-call | tf_op jit(solution)/shard_map/pallas_call | solution.py:184
  71.1 16.1 %all_to_all.11 = f32[128,1,128]{2,1,0:T(1,128)S(1)} all-to-all(f32[128,1,128]{2,1,0:T(1,128)S(1)} %bitcast.9), channel_id=1, replica_groups=mesh['dp'=128,'helper'=2] {'dp'}, dimensions={0} | all-to-all | bytes 131072 | tf_op jit(solution)/shard_map/all_to_all | solution.py:193
  87.2 0.0 copy-done.2
  87.2 0.8 shard_map.40
Async XLA Ops:
  0.0 1.1 %copy-start = (bf16[384,1024]{1,0:T(8,128)(2,1)S(1)}, bf16[384,1024]{1,0:T(8,128)(2,1)}, u32[]{:S(2)}) copy-start(bf16[384,1024]{1,0:T(8,128)(2,1)} %x_hbm.1) | copy-start | bytes 2359300
  1.1 0.7 copy-start.1
  1.8 0.7 copy-start.3
  63.6 5.6 %collective-permute-start = (bf16[6400,128]{1,0:T(8,128)(2,1)S(1)}, bf16[6400,128]{1,0:T(8,128)(2,1)S(1)}, u32[]{:S(2)}, u32[]{:S(2)}) collective-permute-start(bf16[6400,128]{1,0:T(8,128)(2,1)S(1)} %bitcast.6), channel_id=1, source_target_pairs={{0,1},{1,0},{2,3},{3,2},{4,5},{5,4},{6,7},{7,6},{8,9},{9,8},{10,11... | collective-permute-start | bytes 4915208 | tf_op jit(solution)/shard_map/ppermute | solution.py:174
  69.1 18.0 %copy-start.2 = (s32[384]{0:T(512)S(1)}, s32[384]{0:T(512)}, u32[]{:S(2)}) copy-start(s32[384]{0:T(512)} %cluster_ref.1) | copy-start | bytes 4612

commit v3 on v2

--- a/solution.py
+++ b/solution.py
@@ -167,7 +167,7 @@
         [pltpu.VMEM(x.shape, x.dtype) for x in (cluster, member_order, embedding)]
         + [wide, pltpu.SemaphoreType.DMA((3,))],
         [pl.BlockSpec(memory_space=pltpu.HBM)] * 3,
-    )(cluster, member_order, embedding)
+    )(*(pltpu.with_memory_space_constraint(x, pltpu.HBM) for x in (cluster, member_order, embedding)))
     arrived = lax.all_to_all(
         packed.reshape(owners, block // 2, 2, LANES), "dp", split_axis=0, concat_axis=0, tiled=True
     ).reshape(owners * block, LANES)

time: 88.2 us -> 86.3 us (0.978)
  local copies, waits for them, and re-layouts: 2.5 us -> 0.01 us
    unnamed x8 -> x2, local copies, waits for them, and re-layouts: 2.5 us -> 0.01 us
where the time goes in v3:
time: 86.3 us; the launch traced here: 86.1 us
  blocking collectives  75.3 us (87%)
  Pallas kernels  7.07 us (8%)
  starting transfers between devices  2.45 us (3%)
  waiting for transfers between devices  1.28 us (1%)
    all_to_all x1, blocking collectives, per_device(): lax.all_to_all(packed.reshape(owners, block // 2, 2, LANES), 'dp', split_...  59.2 us
    all_to_all x1, blocking collectives, per_device(): lax.all_to_all(nearest.reshape(owners, 1, LANES), 'dp', split_axis=0, con...  16.1 us
    pallas_call x1, Pallas kernels, per_device(): call(functools.partial(pack_kernel, owners, cap), shape((owners * block,...  2.5 us
    ppermute x1, starting transfers between devices, per_device(): other = lax.ppermute(arrived, 'helper', [(0, 1), (1, 0)])  2.45 us
    pallas_call x1, Pallas kernels, per_device(): call(functools.partial(other_kernel, owners, cap), shape((owners, LANES),...  1.93 us
    pallas_call x1, Pallas kernels, per_device(): call(functools.partial(own_kernel, owners, cap), (shape((owners * cap, fe...  1.84 us
  transfers between devices with their start and end apart: 1, of which 1 were waited for; matrix products, arithmetic and copies ran while one was open for 0% of the time, Pallas kernels for 2%

profile of v3, /device:TPU:1, one launch (start us, length us, event | category | flops | bytes accessed | tf_op | source)
XLA Modules:
  0.0 86.1 jit_solution(13700659379146952651)
XLA Ops:
  0.0 2.5 %shard_map.37 = bf16[6400,128]{1,0:T(8,128)(2,1)S(1)} custom-call(s32[384]{0:T(512)} %cluster_ref.1, s32[384]{0:T(512)} %order_hbm.1, bf16[384,1024]{1,0:T(8,128)(2,1)} %x_hbm.1), custom_call_target="tpu_custom_call" | custom-call | tf_op jit(solution)/shard_map/pallas_call | solution.py:164
  2.5 59.2 %all_to_all.10 = bf16[128,25,2,128]{3,2,1,0:T(2,128)(2,1)S(1)} all-to-all(bf16[128,25,2,128]{3,2,1,0:T(2,128)(2,1)S(1)} %bitcast.8), channel_id=1, replica_groups=mesh['dp'=128,'helper'=2] {'dp'}, dimensions={0} | all-to-all | bytes 3276800 | tf_op jit(solution)/shard_map/all_to_all | solution.py:171
  61.7 2.4 %collective-permute-start = (bf16[6400,128]{1,0:T(8,128)(2,1)S(1)}, bf16[6400,128]{1,0:T(8,128)(2,1)S(1)}, u32[]{:S(2)}, u32[]{:S(2)}) collective-permute-start(bf16[6400,128]{1,0:T(8,128)(2,1)S(1)} %bitcast.6), channel_id=1, source_target_pairs={{0,1},{1,0},{2,3},{3,2},{4,5},{5,4},{6,7},{7,6},{8,9},{9,8},{10,11... | collective-permute-start | bytes 4915208 | tf_op jit(solution)/shard_map/ppermute | solution.py:174
  64.2 1.8 %shard_map.38 = (bf16[768,1024]{1,0:T(8,128)(2,1)S(1)}, s32[128,128]{1,0:T(8,128)S(1)}, f32[8,128]{1,0:T(8,128)S(1)}) custom-call(bf16[6400,128]{1,0:T(8,128)(2,1)S(1)} %bitcast.7), custom_call_target="tpu_custom_call" | custom-call | tf_op jit(solution)/shard_map/pallas_call | solution.py:175
  66.0 1.3 %collective-permute-done.block_ref = bf16[6400,128]{1,0:T(8,128)(2,1)S(1)} collective-permute-done((bf16[6400,128]{1,0:T(8,128)(2,1)S(1)}, bf16[6400,128]{1,0:T(8,128)(2,1)S(1)}, u32[]{:S(2)}, u32[]{:S(2)}) %collective-permute-start) | collective-permute-done | bytes 1638432 | tf_op jit(solution)/shard_map/ppermute | solution.py:174
  67.3 0.0 copy-start
  67.3 1.9 %shard_map.39 = f32[128,128]{1,0:T(8,128)S(1)} custom-call(bf16[6400,128]{1,0:T(8,128)(2,1)S(1)} %collective-permute-done.block_ref, bf16[768,1024]{1,0:T(8,128)(2,1)S(1)} %get-tuple-element.8.own_ref, s32[128,128]{1,0:T(8,128)S(1)} %get-tuple-element.9.own_value_ref, f32[8,128]{1,0:T(8,128)S(1)} %get-tuple-element.10.own_best_ref), custom_call_target="tpu_custom_call" | custom-call | tf_op jit(solution)/shard_map/pallas_call | solution.py:184
  69.2 16.1 %all_to_all.11 = f32[128,1,128]{2,1,0:T(1,128)S(1)} all-to-all(f32[128,1,128]{2,1,0:T(1,128)S(1)} %bitcast.9), channel_id=1, replica_groups=mesh['dp'=128,'helper'=2] {'dp'}, dimensions={0} | all-to-all | bytes 131072 | tf_op jit(solution)/shard_map/all_to_all | solution.py:193
  85.3 0.0 copy-done
  85.3 0.8 shard_map.40
Async XLA Ops:
  61.7 5.6 %collective-permute-start = (bf16[6400,128]{1,0:T(8,128)(2,1)S(1)}, bf16[6400,128]{1,0:T(8,128)(2,1)S(1)}, u32[]{:S(2)}, u32[]{:S(2)}) collective-permute-start(bf16[6400,128]{1,0:T(8,128)(2,1)S(1)} %bitcast.6), channel_id=1, source_target_pairs={{0,1},{1,0},{2,3},{3,2},{4,5},{5,4},{6,7},{7,6},{8,9},{9,8},{10,11... | collective-permute-start | bytes 4915208 | tf_op jit(solution)/shard_map/ppermute | solution.py:174
  67.3 18.0 %copy-start = (s32[384]{0:T(512)S(1)}, s32[384]{0:T(512)}, u32[]{:S(2)}) copy-start(s32[384]{0:T(512)} %cluster_ref.1) | copy-start | bytes 4612

commit v4 on v3

--- a/solution.py
+++ b/solution.py
@@ -12,6 +12,26 @@
 SIDE = 8
 CLASS = 1 << 17
 VMEM_LIMIT = 48 << 20
+GRID = (4, 4, 8)
+
+
+def chip_order(owners):
+    opposite = 0
+    for size in GRID:
+        opposite = opposite * size + size // 2
+    bits = owners.bit_length() - 1
+    return [opposite ^ int(f"{i:0{bits}b}"[::-1], 2) for i in range(owners)]
+
+
+def exchange(blocks, owners):
+    return lax.all_to_all(
+        blocks,
+        "dp",
+        split_axis=0,
+        concat_axis=0,
+        axis_index_groups=[chip_order(owners)],
+        tiled=True,
+    )
 
 
 def routing(cluster, owners):
@@ -60,16 +80,16 @@
             (((1,), (1,)), ((), ())),
             preferred_element_type=jnp.float32,
         )
+    picks = jnp.concatenate([member & (slot == s) for s in range(cap)], axis=0).astype(jnp.bfloat16)
     fetch[2].wait()
     values = x_ref[...].astype(jnp.float32)
     scale = lax.rsqrt(jnp.sum(values * values, axis=1, keepdims=True) + 1e-06)
     normed = (values * scale).astype(jnp.bfloat16)
+    rows = jnp.dot(picks, normed, preferred_element_type=jnp.float32)
     for s in range(cap):
-        pick = (member & (slot == s)).astype(jnp.bfloat16)
-        rows = jnp.dot(pick, normed, preferred_element_type=jnp.float32)
         for j in range(chunks):
             wide[pl.ds(s * chunks + j, owners, stride=block), :] = rows[
-                :, j * LANES : (j + 1) * LANES
+                s * owners : (s + 1) * owners, j * LANES : (j + 1) * LANES
             ]
     out_ref[...] = wide[...].astype(jnp.bfloat16)
 
@@ -88,46 +108,41 @@
     return (digit[0] + 256.0 * middle + 65536.0 * digit[1]).astype(jnp.int32)
 
 
-def best_of(sources, cap, keys_ref, key_value, queries_ref, query_value, best_ref):
+def best_of(cap, keys_ref, key_value, queries_ref, query_value, best_ref):
     turned = query_value.T
+    sources, size = query_value.shape[0], key_value.shape[0]
     step = 2 if cap % 2 == 0 else 1
     for q in range(0, cap, step):
-        queries = queries_ref[q * sources : (q + step) * sources, :]
-        best = [best_ref[q + i : q + i + 1, :] for i in range(step)]
-        for k in range(0, cap, step):
-            scores = lax.dot_general(
-                keys_ref[k * sources : (k + step) * sources, :],
-                queries,
-                (((1,), (1,)), ((), ())),
-                preferred_element_type=jnp.float32,
-            )
-            for i in range(step):
-                mine = turned[q + i : q + i + 1, :]
-                floor = mine & ~(CLASS - 1)
-                for m in range(step):
-                    theirs = key_value[:, k + m : k + m + 1]
-                    allowed = (theirs >= floor) & (theirs < mine)
-                    part = scores[m * sources : (m + 1) * sources, i * sources : (i + 1) * sources]
-                    top = jnp.max(jnp.where(allowed, part, -1.0), axis=0, keepdims=True)
-                    best[i] = jnp.maximum(best[i], top)
+        scores = lax.dot_general(
+            keys_ref[...],
+            queries_ref[q * sources : (q + step) * sources, :],
+            (((1,), (1,)), ((), ())),
+            preferred_element_type=jnp.float32,
+        )
         for i in range(step):
-            best_ref[q + i : q + i + 1, :] = best[i]
-
-
-def own_kernel(sources, cap, block_ref, rows_ref, value_ref, best_ref, wide):
-    value = unpack(sources, cap, block_ref, wide, rows_ref)
-    value_ref[...] = value
+            mine = turned[q + i : q + i + 1, :]
+            floor = mine & ~(CLASS - 1)
+            best = best_ref[q + i : q + i + 1, :]
+            for k in range(cap):
+                theirs = key_value[:, k : k + 1]
+                allowed = (theirs >= floor) & (theirs < mine)
+                part = scores[k * size : (k + 1) * size, i * sources : (i + 1) * sources]
+                top = jnp.max(jnp.where(allowed, part, -1.0), axis=0, keepdims=True)
+                best = jnp.maximum(best, top)
+            best_ref[q + i : q + i + 1, :] = best
+
+
+def own_kernel(cap, block_ref, rows_ref, value_ref, best_ref, wide):
+    value_ref[...] = unpack(value_ref.shape[0], cap, block_ref, wide, rows_ref)
     best_ref[...] = jnp.full(best_ref.shape, -1.0, jnp.float32)
-    best_of(sources, cap, rows_ref, value, rows_ref, value, best_ref)
-
-
-def other_kernel(
-    sources, cap, block_ref, own_ref, own_value_ref, own_best_ref, out_ref, wide, rows, best
-):
-    value = unpack(sources, cap, block_ref, wide, rows)
+    best_of(cap, rows_ref, value_ref[...], rows_ref, value_ref[...], best_ref)
+
+
+def other_kernel(cap, block_ref, own_ref, own_value_ref, before_ref, out_ref, wide, rows, best):
+    value = unpack(rows.shape[0] // cap, cap, block_ref, wide, rows)
     best[...] = jnp.full(best.shape, -1.0, jnp.float32)
-    best[: own_best_ref.shape[0], :] = own_best_ref[...]
-    best_of(sources, cap, rows, value, own_ref, own_value_ref[...], best)
+    best[: before_ref.shape[0], :] = before_ref[...]
+    best_of(cap, rows, value, own_ref, own_value_ref[...], best)
     out_ref[...] = best[...].T
 
 
@@ -168,12 +183,12 @@
         + [wide, pltpu.SemaphoreType.DMA((3,))],
         [pl.BlockSpec(memory_space=pltpu.HBM)] * 3,
     )(*(pltpu.with_memory_space_constraint(x, pltpu.HBM) for x in (cluster, member_order, embedding)))
-    arrived = lax.all_to_all(
-        packed.reshape(owners, block // 2, 2, LANES), "dp", split_axis=0, concat_axis=0, tiled=True
-    ).reshape(owners * block, LANES)
+    arrived = exchange(packed.reshape(owners, block // 2, 2, LANES), owners).reshape(
+        owners * block, LANES
+    )
     other = lax.ppermute(arrived, "helper", [(0, 1), (1, 0)])
     rows, value, best = call(
-        functools.partial(own_kernel, owners, cap),
+        functools.partial(own_kernel, cap),
         (
             shape((owners * cap, feature), jnp.bfloat16),
             shape((owners, LANES), jnp.int32),
@@ -182,7 +197,7 @@
         [wide],
     )(arrived)
     nearest = call(
-        functools.partial(other_kernel, owners, cap),
+        functools.partial(other_kernel, cap),
         shape((owners, LANES), jnp.float32),
         [
             wide,
@@ -190,9 +205,7 @@
             pltpu.VMEM((LANES, owners), jnp.float32),
         ],
     )(other, rows, value, best)
-    returned = lax.all_to_all(
-        nearest.reshape(owners, 1, LANES), "dp", split_axis=0, concat_axis=0, tiled=True
-    ).reshape(owners, LANES)
+    returned = exchange(nearest.reshape(owners, 1, LANES), owners).reshape(owners, LANES)
     return call(functools.partial(pick_kernel, owners, cap), shape((count,), jnp.float32))(
         cluster, returned
     )

time: 86.3 us -> 78.6 us (0.911)
  blocking collectives: 75.3 us -> 68.4 us
    all_to_all x2, blocking collectives: 75.3 us -> 68.4 us  [exchange(): lax.all_to_all(blocks, 'dp', split_axis=0, concat_axis=0, axis_index_grou...]
where the time goes in v4:
time: 78.6 us; the launch traced here: 78.3 us
  blocking collectives  68.4 us (87%)
  Pallas kernels  6.82 us (9%)
  starting transfers between devices  1.72 us (2%)
  waiting for transfers between devices  1.32 us (2%)
    all_to_all x2, blocking collectives, exchange(): lax.all_to_all(blocks, 'dp', split_axis=0, concat_axis=0, axis_index_grou...  68.4 us
    pallas_call x1, Pallas kernels, per_device(): call(functools.partial(pack_kernel, owners, cap), shape((owners * block,...  2.43 us
    pallas_call x1, Pallas kernels, per_device(): call(functools.partial(own_kernel, cap), (shape((owners * cap, feature),...  1.8 us
    pallas_call x1, Pallas kernels, per_device(): call(functools.partial(other_kernel, cap), shape((owners, LANES), jnp.flo...  1.79 us
    ppermute x1, starting transfers between devices, per_device(): other = lax.ppermute(arrived, 'helper', [(0, 1), (1, 0)])  1.72 us
  transfers between devices with their start and end apart: 1, of which 1 were waited for; matrix products, arithmetic and copies ran while one was open for 0% of the time, Pallas kernels for 2%

profile of v4, /device:TPU:1, one launch (start us, length us, event | category | flops | bytes accessed | tf_op | source)
XLA Modules:
  0.0 78.3 jit_solution(15652176767928453464)
XLA Ops:
  0.0 2.4 %shard_map.37 = bf16[6400,128]{1,0:T(8,128)(2,1)S(1)} custom-call(s32[384]{0:T(512)} %cluster_ref.1, s32[384]{0:T(512)} %order_hbm.1, bf16[384,1024]{1,0:T(8,128)(2,1)} %x_hbm.1), custom_call_target="tpu_custom_call" | custom-call | tf_op jit(solution)/shard_map/pallas_call | solution.py:179
  2.4 52.8 %all_to_all.10 = bf16[128,25,2,128]{3,2,1,0:T(2,128)(2,1)S(1)} all-to-all(bf16[128,25,2,128]{3,2,1,0:T(2,128)(2,1)S(1)} %bitcast.8), channel_id=1, replica_groups={{168,40,232,104,136,8,200,72,184,56,248,120,152,24,216,88,160,32,224,96..., dimensions={0} | all-to-all | bytes 3276800 | tf_op jit(solution)/shard_map/all_to_all | solution.py:27
  55.3 1.7 %collective-permute-start = (bf16[6400,128]{1,0:T(8,128)(2,1)S(1)}, bf16[6400,128]{1,0:T(8,128)(2,1)S(1)}, u32[]{:S(2)}, u32[]{:S(2)}) collective-permute-start(bf16[6400,128]{1,0:T(8,128)(2,1)S(1)} %bitcast.6), channel_id=1, source_target_pairs={{0,1},{1,0},{2,3},{3,2},{4,5},{5,4},{6,7},{7,6},{8,9},{9,8},{10,11... | collective-permute-start | bytes 4915208 | tf_op jit(solution)/shard_map/ppermute | solution.py:189
  57.0 1.8 %shard_map.38 = (bf16[768,1024]{1,0:T(8,128)(2,1)S(1)}, s32[128,128]{1,0:T(8,128)S(1)}, f32[8,128]{1,0:T(8,128)S(1)}) custom-call(bf16[6400,128]{1,0:T(8,128)(2,1)S(1)} %bitcast.7), custom_call_target="tpu_custom_call" | custom-call | tf_op jit(solution)/shard_map/pallas_call | solution.py:190
  58.8 1.3 %collective-permute-done.block_ref = bf16[6400,128]{1,0:T(8,128)(2,1)S(1)} collective-permute-done((bf16[6400,128]{1,0:T(8,128)(2,1)S(1)}, bf16[6400,128]{1,0:T(8,128)(2,1)S(1)}, u32[]{:S(2)}, u32[]{:S(2)}) %collective-permute-start) | collective-permute-done | bytes 1638432 | tf_op jit(solution)/shard_map/ppermute | solution.py:189
  60.1 0.0 copy-start
  60.1 1.8 %shard_map.39 = f32[128,128]{1,0:T(8,128)S(1)} custom-call(bf16[6400,128]{1,0:T(8,128)(2,1)S(1)} %collective-permute-done.block_ref, bf16[768,1024]{1,0:T(8,128)(2,1)S(1)} %get-tuple-element.8.own_ref, s32[128,128]{1,0:T(8,128)S(1)} %get-tuple-element.9.own_value_ref, f32[8,128]{1,0:T(8,128)S(1)} %get-tuple-element.10.before_ref), custom_call_target="tpu_custom_call" | custom-call | tf_op jit(solution)/shard_map/pallas_call | solution.py:199
  61.9 15.5 %all_to_all.11 = f32[128,1,128]{2,1,0:T(1,128)S(1)} all-to-all(f32[128,1,128]{2,1,0:T(1,128)S(1)} %bitcast.9), channel_id=1, replica_groups={{168,40,232,104,136,8,200,72,184,56,248,120,152,24,216,88,160,32,224,96..., dimensions={0} | all-to-all | bytes 131072 | tf_op jit(solution)/shard_map/all_to_all | solution.py:27
  77.5 0.0 copy-done
  77.5 0.8 %shard_map.40 = f32[384]{0:T(512)} custom-call(s32[384]{0:T(512)S(1)} %copy-done, f32[128,128]{1,0:T(8,128)S(1)} %bitcast.10), custom_call_target="tpu_custom_call" | custom-call | tf_op jit(solution)/shard_map/pallas_call | solution.py:209
Async XLA Ops:
  55.3 4.8 %collective-permute-start = (bf16[6400,128]{1,0:T(8,128)(2,1)S(1)}, bf16[6400,128]{1,0:T(8,128)(2,1)S(1)}, u32[]{:S(2)}, u32[]{:S(2)}) collective-permute-start(bf16[6400,128]{1,0:T(8,128)(2,1)S(1)} %bitcast.6), channel_id=1, source_target_pairs={{0,1},{1,0},{2,3},{3,2},{4,5},{5,4},{6,7},{7,6},{8,9},{9,8},{10,11... | collective-permute-start | bytes 4915208 | tf_op jit(solution)/shard_map/ppermute | solution.py:189
  60.1 17.4 %copy-start = (s32[384]{0:T(512)S(1)}, s32[384]{0:T(512)}, u32[]{:S(2)}) copy-start(s32[384]{0:T(512)} %cluster_ref.1) | copy-start | bytes 4612

commit v5 on v4

--- a/solution.py
+++ b/solution.py
@@ -12,6 +12,7 @@
 SIDE = 8
 CLASS = 1 << 17
 VMEM_LIMIT = 48 << 20
+PARTS = (64, 64)
 GRID = (4, 4, 8)
 
 
@@ -132,18 +133,25 @@
             best_ref[q + i : q + i + 1, :] = best
 
 
+def split_kernel(block_ref, *part_refs):
+    start = 0
+    for part_ref in part_refs:
+        part_ref[...] = block_ref[start : start + part_ref.shape[0], :]
+        start += part_ref.shape[0]
+
+
 def own_kernel(cap, block_ref, rows_ref, value_ref, best_ref, wide):
     value_ref[...] = unpack(value_ref.shape[0], cap, block_ref, wide, rows_ref)
     best_ref[...] = jnp.full(best_ref.shape, -1.0, jnp.float32)
     best_of(cap, rows_ref, value_ref[...], rows_ref, value_ref[...], best_ref)
 
 
-def other_kernel(cap, block_ref, own_ref, own_value_ref, before_ref, out_ref, wide, rows, best):
+def other_kernel(last, cap, block_ref, own_ref, own_value_ref, before_ref, out_ref, wide, rows, best):
     value = unpack(rows.shape[0] // cap, cap, block_ref, wide, rows)
     best[...] = jnp.full(best.shape, -1.0, jnp.float32)
     best[: before_ref.shape[0], :] = before_ref[...]
     best_of(cap, rows, value, own_ref, own_value_ref[...], best)
-    out_ref[...] = best[...].T
+    out_ref[...] = best[...].T if last else best[: out_ref.shape[0], :]
 
 
 def pick_kernel(owners, cap, cluster_ref, result_ref, out_ref):
@@ -186,7 +194,10 @@
     arrived = exchange(packed.reshape(owners, block // 2, 2, LANES), owners).reshape(
         owners * block, LANES
     )
-    other = lax.ppermute(arrived, "helper", [(0, 1), (1, 0)])
+    parts = [shape((size * block, LANES), jnp.bfloat16) for size in PARTS]
+    others = [
+        lax.ppermute(rows, "helper", [(0, 1), (1, 0)]) for rows in call(split_kernel, parts)(arrived)
+    ]
     rows, value, best = call(
         functools.partial(own_kernel, cap),
         (
@@ -196,16 +207,18 @@
         ),
         [wide],
     )(arrived)
-    nearest = call(
-        functools.partial(other_kernel, cap),
-        shape((owners, LANES), jnp.float32),
-        [
-            wide,
-            pltpu.VMEM((owners * cap, feature), jnp.bfloat16),
-            pltpu.VMEM((LANES, owners), jnp.float32),
-        ],
-    )(other, rows, value, best)
-    returned = exchange(nearest.reshape(owners, 1, LANES), owners).reshape(owners, LANES)
+    for p, (size, other) in enumerate(zip(PARTS, others)):
+        last = p == len(PARTS) - 1
+        best = call(
+            functools.partial(other_kernel, last, cap),
+            shape((owners, LANES) if last else (8, owners), jnp.float32),
+            [
+                pltpu.VMEM((size * block, LANES), jnp.float32),
+                pltpu.VMEM((size * cap, feature), jnp.bfloat16),
+                pltpu.VMEM((LANES, owners), jnp.float32),
+            ],
+        )(other, rows, value, best)
+    returned = exchange(best.reshape(owners, 1, LANES), owners).reshape(owners, LANES)
     return call(functools.partial(pick_kernel, owners, cap), shape((count,), jnp.float32))(
         cluster, returned
     )

time: 78.6 us -> 78.1 us (level)
  waiting for transfers between devices: 1.32 us -> 0.26 us
    ppermute x1 -> x2, waiting for transfers between devices: 1.32 us -> 0.26 us  [per_device(): lax.ppermute(rows, 'helper', [(0, 1), (1, 0)])]
    pallas_call x1 -> x3, Pallas kernels: 1.79 us -> 2.15 us  [the longest x2 2.04 us: per_device(): call(functools.partial(other_kernel, last, cap), shape((owners, LANES) if...]
    ppermute x1 -> x2, starting transfers between devices: 1.72 us -> 1.9 us  [per_device(): lax.ppermute(rows, 'helper', [(0, 1), (1, 0)])]
  transfers between devices with their start and end apart: 1 -> 2, of which waited for: 1 -> 2; matrix products, arithmetic and copies ran while one was open for 0% -> 0% of each run, Pallas kernels for 2% -> 4%
where the time goes in v5:
time: 78.1 us; the launch traced here: 77.7 us
  blocking collectives  68.4 us (88%)
  Pallas kernels  7.15 us (9%)
  starting transfers between devices  1.9 us (2%)
    all_to_all x2, blocking collectives, exchange(): lax.all_to_all(blocks, 'dp', split_axis=0, concat_axis=0, axis_index_grou...  68.4 us
    pallas_call x1, Pallas kernels, per_device(): call(functools.partial(pack_kernel, owners, cap), shape((owners * block,...  2.43 us
    pallas_call x2, Pallas kernels, per_device(): call(functools.partial(other_kernel, last, cap), shape((owners, LANES) if...  2.04 us
    ppermute x2, starting transfers between devices, per_device(): lax.ppermute(rows, 'helper', [(0, 1), (1, 0)])  1.9 us
    pallas_call x1, Pallas kernels, per_device(): call(functools.partial(own_kernel, cap), (shape((owners * cap, feature),...  1.78 us
  transfers between devices with their start and end apart: 2, of which 2 were waited for; matrix products, arithmetic and copies ran while one was open for 0% of the time, Pallas kernels for 4%

profile of v5, /device:TPU:1, one launch (start us, length us, event | category | flops | bytes accessed | tf_op | source)
XLA Modules:
  0.0 77.7 jit_solution(11935912334679525463)
XLA Ops:
  0.0 2.4 %shard_map.37 = bf16[6400,128]{1,0:T(8,128)(2,1)S(1)} custom-call(s32[384]{0:T(512)} %cluster_ref.1, s32[384]{0:T(512)} %order_hbm.1, bf16[384,1024]{1,0:T(8,128)(2,1)} %x_hbm.1), custom_call_target="tpu_custom_call" | custom-call | tf_op jit(solution)/shard_map/pallas_call | solution.py:187
  2.4 52.8 %all_to_all.10 = bf16[128,25,2,128]{3,2,1,0:T(2,128)(2,1)S(1)} all-to-all(bf16[128,25,2,128]{3,2,1,0:T(2,128)(2,1)S(1)} %bitcast.8), channel_id=1, replica_groups={{168,40,232,104,136,8,200,72,184,56,248,120,152,24,216,88,160,32,224,96..., dimensions={0} | all-to-all | bytes 3276800 | tf_op jit(solution)/shard_map/all_to_all | solution.py:28
  55.3 0.1 shard_map.38
  55.4 1.8 %collective-permute-start.1 = (bf16[3200,128]{1,0:T(8,128)(2,1)S(1)}, bf16[3200,128]{1,0:T(8,128)(2,1)S(1)}, u32[]{:S(2)}, u32[]{:S(2)}) collective-permute-start(bf16[3200,128]{1,0:T(8,128)(2,1)S(1)} %get-tuple-element.13), channel_id=1, source_target_pairs={{0,1},{1,0},{2,3},{3,2},{4,5},{5,4},{6,7},{7,6},{8,9},{9,8},{10,11... | collective-permute-start | bytes 2457608 | tf_op jit(solution)/shard_map/ppermute | solution.py:199
  57.2 0.1 collective-permute-start
  57.3 1.8 %shard_map.39 = (bf16[768,1024]{1,0:T(8,128)(2,1)S(1)}, s32[128,128]{1,0:T(8,128)S(1)}, f32[8,128]{1,0:T(8,128)S(1)}) custom-call(bf16[6400,128]{1,0:T(8,128)(2,1)S(1)} %bitcast.7), custom_call_target="tpu_custom_call" | custom-call | tf_op jit(solution)/shard_map/pallas_call | solution.py:201
  59.1 0.1 collective-permute-done.1.block_ref
  59.1 1.0 %shard_map.40.before_ref = f32[8,128]{1,0:T(8,128)S(1)} custom-call(bf16[3200,128]{1,0:T(8,128)(2,1)S(1)} %collective-permute-done.1.block_ref, bf16[768,1024]{1,0:T(8,128)(2,1)S(1)} %get-tuple-element.11.own_ref, s32[128,128]{1,0:T(8,128)S(1)} %get-tuple-element.12.own_value_ref, f32[8,128]{1,0:T(8,128)S(1)} %get-tuple-element.14.before_ref), custom_call_target="tpu_custom_call" | custom-call | tf_op jit(solution)/shard_map/pallas_call | solution.py:212
  60.1 0.0 copy-start
  60.1 0.2 collective-permute-done.block_ref
  60.3 1.1 %shard_map.41 = f32[128,128]{1,0:T(8,128)S(1)} custom-call(bf16[3200,128]{1,0:T(8,128)(2,1)S(1)} %collective-permute-done.block_ref, bf16[768,1024]{1,0:T(8,128)(2,1)S(1)} %get-tuple-element.11.own_ref, s32[128,128]{1,0:T(8,128)S(1)} %get-tuple-element.12.own_value_ref, f32[8,128]{1,0:T(8,128)S(1)} %shard_map.40.before_ref), custom_call_target="tpu_custom_call" | custom-call | tf_op jit(solution)/shard_map/pallas_call | solution.py:212
  61.4 15.5 %all_to_all.11 = f32[128,1,128]{2,1,0:T(1,128)S(1)} all-to-all(f32[128,1,128]{2,1,0:T(1,128)S(1)} %bitcast.9), channel_id=1, replica_groups={{168,40,232,104,136,8,200,72,184,56,248,120,152,24,216,88,160,32,224,96..., dimensions={0} | all-to-all | bytes 131072 | tf_op jit(solution)/shard_map/all_to_all | solution.py:28
  76.9 0.0 copy-done
  76.9 0.8 %shard_map.42 = f32[384]{0:T(512)} custom-call(s32[384]{0:T(512)S(1)} %copy-done, f32[128,128]{1,0:T(8,128)S(1)} %bitcast.10), custom_call_target="tpu_custom_call" | custom-call | tf_op jit(solution)/shard_map/pallas_call | solution.py:222
Async XLA Ops:
  55.4 3.8 %collective-permute-start.1 = (bf16[3200,128]{1,0:T(8,128)(2,1)S(1)}, bf16[3200,128]{1,0:T(8,128)(2,1)S(1)}, u32[]{:S(2)}, u32[]{:S(2)}) collective-permute-start(bf16[3200,128]{1,0:T(8,128)(2,1)S(1)} %get-tuple-element.13), channel_id=1, source_target_pairs={{0,1},{1,0},{2,3},{3,2},{4,5},{5,4},{6,7},{7,6},{8,9},{9,8},{10,11... | collective-permute-start | bytes 2457608 | tf_op jit(solution)/shard_map/ppermute | solution.py:199
  57.2 3.1 %collective-permute-start = (bf16[3200,128]{1,0:T(8,128)(2,1)S(1)}, bf16[3200,128]{1,0:T(8,128)(2,1)S(1)}, u32[]{:S(2)}, u32[]{:S(2)}) collective-permute-start(bf16[3200,128]{1,0:T(8,128)(2,1)S(1)} %get-tuple-element.10), channel_id=1, source_target_pairs={{0,1},{1,0},{2,3},{3,2},{4,5},{5,4},{6,7},{7,6},{8,9},{9,8},{10,11... | collective-permute-start | bytes 2457608 | tf_op jit(solution)/shard_map/ppermute | solution.py:199
  60.1 16.8 %copy-start = (s32[384]{0:T(512)S(1)}, s32[384]{0:T(512)}, u32[]{:S(2)}) copy-start(s32[384]{0:T(512)} %cluster_ref.1) | copy-start | bytes 4612

commit v6 on v5

--- a/solution.py
+++ b/solution.py
@@ -35,21 +35,23 @@
     )
 
 
-def routing(cluster, owners):
+def earlier_documents(count):
+    row = lax.broadcasted_iota(jnp.int32, (count, count), 0)
+    return (row < lax.broadcasted_iota(jnp.int32, (count, count), 1)).astype(jnp.bfloat16)
+
+
+def routing(cluster, owners, before):
     count = cluster.shape[1]
     owner = lax.rem(cluster, owners)
     member = lax.broadcasted_iota(jnp.int32, (owners, count), 0) == owner
-    before = lax.broadcasted_iota(jnp.int32, (count, count), 0) < lax.broadcasted_iota(
-        jnp.int32, (count, count), 1
-    )
     ones = member.astype(jnp.bfloat16)
-    earlier = jnp.dot(ones, before.astype(jnp.bfloat16), preferred_element_type=jnp.float32)
+    earlier = jnp.dot(ones, before, preferred_element_type=jnp.float32)
     slot = jnp.sum(jnp.where(member, earlier, 0.0), axis=0, keepdims=True).astype(jnp.int32)
     return member, slot
 
 
 def pack_kernel(
-    owners, cap, cluster_hbm, order_hbm, x_hbm, out_ref, cluster_ref, order_ref, x_ref, wide, arrived
+    owners, cap, cluster_hbm, order_hbm, x_hbm, out_ref, place_ref, cluster_ref, order_ref, x_ref, wide, arrived
 ):
     given = (cluster_hbm, order_hbm, x_hbm)
     fetch = [
@@ -58,16 +60,19 @@
     ]
     for copy in fetch:
         copy.start()
+    count, feature = x_ref.shape
+    before = earlier_documents(count)
     fetch[0].wait()
-    fetch[1].wait()
-    count, feature = x_ref.shape
     chunks = feature // LANES
     block = cap * chunks + META
     cluster = cluster_ref[...].reshape(1, count)
-    order = order_ref[...].reshape(1, count)
-    member, slot = routing(cluster, owners)
+    member, slot = routing(cluster, owners, before)
+    place_ref[0:1, :] = lax.rem(cluster, owners)
+    place_ref[1:2, :] = slot
     ones = member.astype(jnp.bfloat16)
     lane = lax.broadcasted_iota(jnp.int32, (LANES, count), 0)
+    fetch[1].wait()
+    order = order_ref[...].reshape(1, count)
     low, middle = order & 255, (order >> 8) & 255
     high = (order >> 16) + 2 * lax.div(cluster, owners) + 8
     spread = (
@@ -133,6 +138,46 @@
             best_ref[q + i : q + i + 1, :] = best
 
 
+def best_among(cap, rows_ref, value, best_ref):
+    sources = value.shape[0]
+    turned = value.T
+    step = 2 if cap % 2 == 0 else 1
+    down = [jnp.broadcast_to(value[:, k : k + 1], (sources, sources)) for k in range(cap)]
+    across = [jnp.full((1, sources), -1.0, jnp.float32) for _ in range(cap)]
+    along = [None] * cap
+    for q in range(0, cap, step):
+        for k in range(0, q + 1, step):
+            scores = lax.dot_general(
+                rows_ref[k * sources : (k + step) * sources, :],
+                rows_ref[q * sources : (q + step) * sources, :],
+                (((1,), (1,)), ((), ())),
+                preferred_element_type=jnp.float32,
+            )
+            for i in range(q, q + step):
+                mine = turned[i : i + 1, :]
+                for m in range(k, k + step):
+                    theirs = down[m]
+                    part = scores[
+                        (m - k) * sources : (m - k + 1) * sources,
+                        (i - q) * sources : (i - q + 1) * sources,
+                    ]
+                    allowed = (theirs >= (mine & ~(CLASS - 1))) & (theirs < mine)
+                    top = jnp.max(jnp.where(allowed, part, -1.0), axis=0, keepdims=True)
+                    across[i] = jnp.maximum(across[i], top)
+                    if k < q:
+                        allowed = (mine >= (theirs & ~(CLASS - 1))) & (mine < theirs)
+                        top = jnp.where(allowed, part, -1.0)
+                        along[m] = top if along[m] is None else jnp.maximum(along[m], top)
+    lane = lax.broadcasted_iota(jnp.int32, (sources, LANES), 1)
+    columns = jnp.full((sources, LANES), -1.0, jnp.float32)
+    for m, top in enumerate(along):
+        if top is not None:
+            columns = jnp.where(lane == m, jnp.max(top, axis=1, keepdims=True), columns)
+    best_ref[...] = columns.T[: best_ref.shape[0], :]
+    for i in range(cap):
+        best_ref[i : i + 1, :] = jnp.maximum(best_ref[i : i + 1, :], across[i])
+
+
 def split_kernel(block_ref, *part_refs):
     start = 0
     for part_ref in part_refs:
@@ -142,8 +187,7 @@
 
 def own_kernel(cap, block_ref, rows_ref, value_ref, best_ref, wide):
     value_ref[...] = unpack(value_ref.shape[0], cap, block_ref, wide, rows_ref)
-    best_ref[...] = jnp.full(best_ref.shape, -1.0, jnp.float32)
-    best_of(cap, rows_ref, value_ref[...], rows_ref, value_ref[...], best_ref)
+    best_among(cap, rows_ref, value_ref[...], best_ref)
 
 
 def other_kernel(last, cap, block_ref, own_ref, own_value_ref, before_ref, out_ref, wide, rows, best):
@@ -154,9 +198,10 @@
     out_ref[...] = best[...].T if last else best[: out_ref.shape[0], :]
 
 
-def pick_kernel(owners, cap, cluster_ref, result_ref, out_ref):
-    count = cluster_ref.shape[0]
-    member, slot = routing(cluster_ref[...].reshape(1, count), owners)
+def pick_kernel(owners, cap, place_ref, result_ref, out_ref):
+    count = place_ref.shape[1]
+    member = lax.broadcasted_iota(jnp.int32, (owners, count), 0) == place_ref[0:1, :]
+    slot = place_ref[1:2, :]
     result = result_ref[...]
     found = jnp.full(slot.shape, -1.0, jnp.float32)
     for s in range(cap):
@@ -184,9 +229,9 @@
     block = cap * feature // LANES + META
     shape = jax.ShapeDtypeStruct
     wide = pltpu.VMEM((owners * block, LANES), jnp.float32)
-    packed = call(
+    packed, place = call(
         functools.partial(pack_kernel, owners, cap),
-        shape((owners * block, LANES), jnp.bfloat16),
+        (shape((owners * block, LANES), jnp.bfloat16), shape((8, count), jnp.int32)),
         [pltpu.VMEM(x.shape, x.dtype) for x in (cluster, member_order, embedding)]
         + [wide, pltpu.SemaphoreType.DMA((3,))],
         [pl.BlockSpec(memory_space=pltpu.HBM)] * 3,
@@ -220,7 +265,7 @@
         )(other, rows, value, best)
     returned = exchange(best.reshape(owners, 1, LANES), owners).reshape(owners, LANES)
     return call(functools.partial(pick_kernel, owners, cap), shape((count,), jnp.float32))(
-        cluster, returned
+        place, returned
     )
 
 

time: 78.1 us -> 78.1 us (level)
  transfers between devices with their start and end apart: 2 -> 2, of which waited for: 2 -> 2; matrix products, arithmetic and copies ran while one was open for 0% -> 0% of each run, Pallas kernels for 4% -> 3%
where the time goes in v6:
time: 78.1 us; the launch traced here: 77.7 us
  blocking collectives  68.4 us (88%)
  Pallas kernels  6.98 us (9%)
  starting transfers between devices  1.9 us (2%)
    all_to_all x2, blocking collectives, exchange(): lax.all_to_all(blocks, 'dp', split_axis=0, concat_axis=0, axis_index_grou...  68.4 us
    pallas_call x1, Pallas kernels, per_device(): call(functools.partial(pack_kernel, owners, cap), (shape((owners * block,...  2.43 us
    pallas_call x2, Pallas kernels, per_device(): call(functools.partial(other_kernel, last, cap), shape((owners, LANES) if...  2.04 us
    ppermute x2, starting transfers between devices, per_device(): lax.ppermute(rows, 'helper', [(0, 1), (1, 0)])  1.9 us
    pallas_call x1, Pallas kernels, per_device(): call(functools.partial(own_kernel, cap), (shape((owners * cap, feature),...  1.63 us
  transfers between devices with their start and end apart: 2, of which 2 were waited for; matrix products, arithmetic and copies ran while one was open for 0% of the time, Pallas kernels for 3%

profile of v6, /device:TPU:1, one launch (start us, length us, event | category | flops | bytes accessed | tf_op | source)
XLA Modules:
  0.0 77.7 jit_solution(7710390509266392293)
XLA Ops:
  0.0 2.4 %shard_map.37 = (bf16[6400,128]{1,0:T(8,128)(2,1)S(1)}, s32[8,384]{1,0:T(8,128)S(1)}) custom-call(s32[384]{0:T(512)} %cluster_hbm.1, s32[384]{0:T(512)} %order_hbm.1, bf16[384,1024]{1,0:T(8,128)(2,1)} %x_hbm.1), custom_call_target="tpu_custom_call" | custom-call | tf_op jit(solution)/shard_map/pallas_call | solution.py:232
  2.4 52.8 %all_to_all.10 = bf16[128,25,2,128]{3,2,1,0:T(2,128)(2,1)S(1)} all-to-all(bf16[128,25,2,128]{3,2,1,0:T(2,128)(2,1)S(1)} %bitcast.8), channel_id=1, replica_groups={{168,40,232,104,136,8,200,72,184,56,248,120,152,24,216,88,160,32,224,96..., dimensions={0} | all-to-all | bytes 3276800 | tf_op jit(solution)/shard_map/all_to_all | solution.py:28
  55.3 0.1 shard_map.38
  55.4 1.8 %collective-permute-start.1 = (bf16[3200,128]{1,0:T(8,128)(2,1)S(1)}, bf16[3200,128]{1,0:T(8,128)(2,1)S(1)}, u32[]{:S(2)}, u32[]{:S(2)}) collective-permute-start(bf16[3200,128]{1,0:T(8,128)(2,1)S(1)} %get-tuple-element.17), channel_id=1, source_target_pairs={{0,1},{1,0},{2,3},{3,2},{4,5},{5,4},{6,7},{7,6},{8,9},{9,8},{10,11... | collective-permute-start | bytes 2457608 | tf_op jit(solution)/shard_map/ppermute | solution.py:244
  57.2 0.1 collective-permute-start
  57.3 1.6 %shard_map.39 = (bf16[768,1024]{1,0:T(8,128)(2,1)S(1)}, s32[128,128]{1,0:T(8,128)S(1)}, f32[8,128]{1,0:T(8,128)S(1)}) custom-call(bf16[6400,128]{1,0:T(8,128)(2,1)S(1)} %bitcast.7), custom_call_target="tpu_custom_call" | custom-call | tf_op jit(solution)/shard_map/pallas_call | solution.py:246
  58.9 0.2 collective-permute-done.1.block_ref
  59.1 1.0 %shard_map.40.before_ref = f32[8,128]{1,0:T(8,128)S(1)} custom-call(bf16[3200,128]{1,0:T(8,128)(2,1)S(1)} %collective-permute-done.1.block_ref, bf16[768,1024]{1,0:T(8,128)(2,1)S(1)} %get-tuple-element.15.own_ref, s32[128,128]{1,0:T(8,128)S(1)} %get-tuple-element.16.own_value_ref, f32[8,128]{1,0:T(8,128)S(1)} %get-tuple-element.18.before_ref), custom_call_target="tpu_custom_call" | custom-call | tf_op jit(solution)/shard_map/pallas_call | solution.py:257
  60.1 0.2 collective-permute-done.block_ref
  60.3 1.1 %shard_map.41 = f32[128,128]{1,0:T(8,128)S(1)} custom-call(bf16[3200,128]{1,0:T(8,128)(2,1)S(1)} %collective-permute-done.block_ref, bf16[768,1024]{1,0:T(8,128)(2,1)S(1)} %get-tuple-element.15.own_ref, s32[128,128]{1,0:T(8,128)S(1)} %get-tuple-element.16.own_value_ref, f32[8,128]{1,0:T(8,128)S(1)} %shard_map.40.before_ref), custom_call_target="tpu_custom_call" | custom-call | tf_op jit(solution)/shard_map/pallas_call | solution.py:257
  61.4 15.5 %all_to_all.11 = f32[128,1,128]{2,1,0:T(1,128)S(1)} all-to-all(f32[128,1,128]{2,1,0:T(1,128)S(1)} %bitcast.9), channel_id=1, replica_groups={{168,40,232,104,136,8,200,72,184,56,248,120,152,24,216,88,160,32,224,96..., dimensions={0} | all-to-all | bytes 131072 | tf_op jit(solution)/shard_map/all_to_all | solution.py:28
  76.9 0.8 shard_map.42
Async XLA Ops:
  55.4 3.8 %collective-permute-start.1 = (bf16[3200,128]{1,0:T(8,128)(2,1)S(1)}, bf16[3200,128]{1,0:T(8,128)(2,1)S(1)}, u32[]{:S(2)}, u32[]{:S(2)}) collective-permute-start(bf16[3200,128]{1,0:T(8,128)(2,1)S(1)} %get-tuple-element.17), channel_id=1, source_target_pairs={{0,1},{1,0},{2,3},{3,2},{4,5},{5,4},{6,7},{7,6},{8,9},{9,8},{10,11... | collective-permute-start | bytes 2457608 | tf_op jit(solution)/shard_map/ppermute | solution.py:244
  57.2 3.1 %collective-permute-start = (bf16[3200,128]{1,0:T(8,128)(2,1)S(1)}, bf16[3200,128]{1,0:T(8,128)(2,1)S(1)}, u32[]{:S(2)}, u32[]{:S(2)}) collective-permute-start(bf16[3200,128]{1,0:T(8,128)(2,1)S(1)} %get-tuple-element.14), channel_id=1, source_target_pairs={{0,1},{1,0},{2,3},{3,2},{4,5},{5,4},{6,7},{7,6},{8,9},{9,8},{10,11... | collective-permute-start | bytes 2457608 | tf_op jit(solution)/shard_map/ppermute | solution.py:244

commit v7 on v6

--- a/solution.py
+++ b/solution.py
@@ -79,13 +79,16 @@
         jnp.where(lane == slot, low, jnp.where(lane == slot + SIDE, middle, 0)),
         jnp.where(lane == slot, high, 0),
     )
+    digits = lax.dot_general(
+        ones,
+        jnp.concatenate(spread, axis=0).astype(jnp.float32).astype(jnp.bfloat16),
+        (((1,), (1,)), ((), ())),
+        preferred_element_type=jnp.float32,
+    )
     for r in range(META):
-        wide[pl.ds(cap * chunks + r, owners, stride=block), :] = lax.dot_general(
-            ones,
-            spread[r].astype(jnp.float32).astype(jnp.bfloat16),
-            (((1,), (1,)), ((), ())),
-            preferred_element_type=jnp.float32,
-        )
+        wide[pl.ds(cap * chunks + r, owners, stride=block), :] = digits[
+            :, r * LANES : (r + 1) * LANES
+        ]
     picks = jnp.concatenate([member & (slot == s) for s in range(cap)], axis=0).astype(jnp.bfloat16)
     fetch[2].wait()
     values = x_ref[...].astype(jnp.float32)

time: 78.1 us -> 78.1 us (level)
  no operation moved by 1% of the time
where the time goes in v7:
time: 78.1 us; the launch traced here: 77.7 us
  blocking collectives  68.4 us (88%)
  Pallas kernels  7.02 us (9%)
  starting transfers between devices  1.9 us (2%)
    all_to_all x2, blocking collectives, exchange(): lax.all_to_all(blocks, 'dp', split_axis=0, concat_axis=0, axis_index_grou...  68.4 us
    pallas_call x1, Pallas kernels, per_device(): call(functools.partial(pack_kernel, owners, cap), (shape((owners * block,...  2.47 us
    pallas_call x2, Pallas kernels, per_device(): call(functools.partial(other_kernel, last, cap), shape((owners, LANES) if...  2.04 us
    ppermute x2, starting transfers between devices, per_device(): lax.ppermute(rows, 'helper', [(0, 1), (1, 0)])  1.9 us
    pallas_call x1, Pallas kernels, per_device(): call(functools.partial(own_kernel, cap), (shape((owners * cap, feature),...  1.63 us
  transfers between devices with their start and end apart: 2, of which 2 were waited for; matrix products, arithmetic and copies ran while one was open for 0% of the time, Pallas kernels for 3%

profile of v7, /device:TPU:1, one launch (start us, length us, event | category | flops | bytes accessed | tf_op | source)
XLA Modules:
  0.0 77.7 jit_solution(13415948113614959841)
XLA Ops:
  0.0 2.5 %shard_map.37 = (bf16[6400,128]{1,0:T(8,128)(2,1)S(1)}, s32[8,384]{1,0:T(8,128)S(1)}) custom-call(s32[384]{0:T(512)} %cluster_hbm.1, s32[384]{0:T(512)} %order_hbm.1, bf16[384,1024]{1,0:T(8,128)(2,1)} %x_hbm.1), custom_call_target="tpu_custom_call" | custom-call | tf_op jit(solution)/shard_map/pallas_call | solution.py:235
  2.5 52.8 %all_to_all.10 = bf16[128,25,2,128]{3,2,1,0:T(2,128)(2,1)S(1)} all-to-all(bf16[128,25,2,128]{3,2,1,0:T(2,128)(2,1)S(1)} %bitcast.8), channel_id=1, replica_groups={{168,40,232,104,136,8,200,72,184,56,248,120,152,24,216,88,160,32,224,96..., dimensions={0} | all-to-all | bytes 3276800 | tf_op jit(solution)/shard_map/all_to_all | solution.py:28
  55.3 0.1 shard_map.38
  55.4 1.8 %collective-permute-start.1 = (bf16[3200,128]{1,0:T(8,128)(2,1)S(1)}, bf16[3200,128]{1,0:T(8,128)(2,1)S(1)}, u32[]{:S(2)}, u32[]{:S(2)}) collective-permute-start(bf16[3200,128]{1,0:T(8,128)(2,1)S(1)} %get-tuple-element.17), channel_id=1, source_target_pairs={{0,1},{1,0},{2,3},{3,2},{4,5},{5,4},{6,7},{7,6},{8,9},{9,8},{10,11... | collective-permute-start | bytes 2457608 | tf_op jit(solution)/shard_map/ppermute | solution.py:247
  57.2 0.1 collective-permute-start
  57.3 1.6 %shard_map.39 = (bf16[768,1024]{1,0:T(8,128)(2,1)S(1)}, s32[128,128]{1,0:T(8,128)S(1)}, f32[8,128]{1,0:T(8,128)S(1)}) custom-call(bf16[6400,128]{1,0:T(8,128)(2,1)S(1)} %bitcast.7), custom_call_target="tpu_custom_call" | custom-call | tf_op jit(solution)/shard_map/pallas_call | solution.py:249
  58.9 0.2 collective-permute-done.1.block_ref
  59.2 1.0 %shard_map.40.before_ref = f32[8,128]{1,0:T(8,128)S(1)} custom-call(bf16[3200,128]{1,0:T(8,128)(2,1)S(1)} %collective-permute-done.1.block_ref, bf16[768,1024]{1,0:T(8,128)(2,1)S(1)} %get-tuple-element.15.own_ref, s32[128,128]{1,0:T(8,128)S(1)} %get-tuple-element.16.own_value_ref, f32[8,128]{1,0:T(8,128)S(1)} %get-tuple-element.18.before_ref), custom_call_target="tpu_custom_call" | custom-call | tf_op jit(solution)/shard_map/pallas_call | solution.py:260
  60.1 0.2 collective-permute-done.block_ref
  60.3 1.1 %shard_map.41 = f32[128,128]{1,0:T(8,128)S(1)} custom-call(bf16[3200,128]{1,0:T(8,128)(2,1)S(1)} %collective-permute-done.block_ref, bf16[768,1024]{1,0:T(8,128)(2,1)S(1)} %get-tuple-element.15.own_ref, s32[128,128]{1,0:T(8,128)S(1)} %get-tuple-element.16.own_value_ref, f32[8,128]{1,0:T(8,128)S(1)} %shard_map.40.before_ref), custom_call_target="tpu_custom_call" | custom-call | tf_op jit(solution)/shard_map/pallas_call | solution.py:260
  61.4 15.5 %all_to_all.11 = f32[128,1,128]{2,1,0:T(1,128)S(1)} all-to-all(f32[128,1,128]{2,1,0:T(1,128)S(1)} %bitcast.9), channel_id=1, replica_groups={{168,40,232,104,136,8,200,72,184,56,248,120,152,24,216,88,160,32,224,96..., dimensions={0} | all-to-all | bytes 131072 | tf_op jit(solution)/shard_map/all_to_all | solution.py:28
  77.0 0.8 shard_map.42
Async XLA Ops:
  55.4 3.8 %collective-permute-start.1 = (bf16[3200,128]{1,0:T(8,128)(2,1)S(1)}, bf16[3200,128]{1,0:T(8,128)(2,1)S(1)}, u32[]{:S(2)}, u32[]{:S(2)}) collective-permute-start(bf16[3200,128]{1,0:T(8,128)(2,1)S(1)} %get-tuple-element.17), channel_id=1, source_target_pairs={{0,1},{1,0},{2,3},{3,2},{4,5},{5,4},{6,7},{7,6},{8,9},{9,8},{10,11... | collective-permute-start | bytes 2457608 | tf_op jit(solution)/shard_map/ppermute | solution.py:247
  57.2 3.1 %collective-permute-start = (bf16[3200,128]{1,0:T(8,128)(2,1)S(1)}, bf16[3200,128]{1,0:T(8,128)(2,1)S(1)}, u32[]{:S(2)}, u32[]{:S(2)}) collective-permute-start(bf16[3200,128]{1,0:T(8,128)(2,1)S(1)} %get-tuple-element.14), channel_id=1, source_target_pairs={{0,1},{1,0},{2,3},{3,2},{4,5},{5,4},{6,7},{7,6},{8,9},{9,8},{10,11... | collective-permute-start | bytes 2457608 | tf_op jit(solution)/shard_map/ppermute | solution.py:247
